TPU v7x, 32 devices: a whole 2x2x4 slice. The times are simulated.
32 devices in a mesh: chan: 4 (over z), sx: 4 (over x, core), sy: 2 (over y).
Axes of the slice: x: 2, y: 2, z: 4, core: 2. Of those that a mesh axis runs over, the one named last changes fastest.
Arguments:
- volume: bfloat16 [4, 16, 64, 256], P('sx', 'sy', None, 'chan'), may hold values from -6 to 6
- kernel: bfloat16 [27, 256, 256], P(None, 'chan'), may hold values from -0.078125 to 0.078125
- grad_out: bfloat16 [4, 16, 64, 256], P('sx', 'sy', None, 'chan'), may hold values from -6 to 6
Outputs:
- out: bfloat16 [4, 16, 64, 256], P('sx', 'sy', None, 'chan')
- grad_input: bfloat16 [4, 16, 64, 256], P('sx', 'sy', None, 'chan')
- grad_kernel: float32 [27, 256, 256], P(None, 'chan')
All inputs are finite; a program needn't handle non-finite values.
Results may differ from a plain program's by a relative error of at most 0.0015.
Values may be sent and summed in bfloat16 or wider, within the bound.
A program may use at most 64 MiB of HBM per device.

v0:
```python
import math

import jax
import jax.numpy as jnp
from jax import lax
from jax.sharding import PartitionSpec as P


def padded_2(shard, sides, width):
    for axis, dim in sides:
        count, length = (lax.axis_size(axis), shard.shape[dim])
        up = [(i, (i + 1) % count) for i in range(count - 1)]
        down = [(j, i) for i, j in up]
        last = lax.slice_in_dim(shard, length - width, length, axis=dim)
        leading = lax.slice_in_dim(shard, 0, width, axis=dim)
        before = lax.ppermute(last, axis, up)
        after = lax.ppermute(leading, axis, down)
        shard = jnp.concatenate([before, shard, after], axis=dim)
    return shard


def body(volume, kernel, grad_out):
    size_x, size_y, size_z, own_in = volume.shape
    total_out = kernel.shape[2]
    cells = size_x * size_y * size_z
    rim = padded_2(volume, (("sx", 0), ("sy", 1)), 1)
    padded = jnp.pad(rim, ((0, 0), (0, 0), (1, 1), (0, 0)))
    offsets = [(index // 9, index // 3 % 3, index % 3) for index in range(27)]
    partial_out = jnp.zeros((cells, total_out), jnp.float32)
    for index in range(27):
        a, b, e = offsets[index]
        window = padded[a : a + size_x, b : b + size_y, e : e + size_z].reshape(cells, own_in)
        partial_out = partial_out + jnp.dot(
            window, kernel[index], preferred_element_type=jnp.float32
        )
    partial_out = partial_out.reshape(size_x, size_y, size_z, total_out)
    out = lax.psum_scatter(partial_out, "chan", scatter_dimension=3, tiled=True).astype(
        jnp.bfloat16
    )
    grad_full = lax.all_gather(grad_out, "chan", axis=3, tiled=True)
    grad_rimmed = padded_2(grad_full, (("sx", 0), ("sy", 1)), 1)
    grad_padded = jnp.pad(grad_rimmed, ((0, 0), (0, 0), (1, 1), (0, 0)))
    flat_grad = grad_full.reshape(cells, total_out)
    back = jnp.zeros((cells, own_in), jnp.float32)
    kernel_terms = []
    for index in range(27):
        a, b, e = offsets[index]
        window = grad_padded[
            2 - a : 2 - a + size_x, 2 - b : 2 - b + size_y, 2 - e : 2 - e + size_z
        ].reshape(cells, total_out)
        back = back + lax.dot_general(
            window, kernel[index], (((1,), (1,)), ((), ())), preferred_element_type=jnp.float32
        )
        in_window = padded[a : a + size_x, b : b + size_y, e : e + size_z].reshape(cells, own_in)
        kernel_terms.append(
            lax.dot_general(
                in_window, flat_grad, (((0,), (0,)), ((), ())), preferred_element_type=jnp.float32
            )
        )
    grad_input = back.reshape(size_x, size_y, size_z, own_in).astype(jnp.bfloat16)
    local_kernel = jnp.stack(kernel_terms)
    summed = lax.psum(local_kernel, ("sx", "sy"))
    all_cells = cells * lax.axis_size("sx") * lax.axis_size("sy")
    grad_kernel = summed / jnp.float32(math.sqrt(all_cells))
    return (out, grad_input, grad_kernel)


def solution(mesh):
    return jax.shard_map(
        body,
        mesh=mesh,
        in_specs=(P("sx", "sy", None, "chan"), P(None, "chan", None), P("sx", "sy", None, "chan")),
        out_specs=(P("sx", "sy", None, "chan"), P("sx", "sy", None, "chan"), P(None, "chan", None)),
        check_vma=False,
    )
```

profile of v0, /device:TPU:0, one launch (start us, length us, event | category | flops | bytes accessed | tf_op | source)
XLA Modules:
  0.0 202.0 jit_solution(9827488505250742948)
XLA Ops:
  10.4 3.0 %collective-permute-start = (bf16[1,8,64,64]{2,3,1,0:T(8,128)(2,1)S(1)}, bf16[1,8,64,64]{2,3,1,0:T(8,128)(2,1)S(1)}, u32[]{:S(2)}, u32[]{:S(2)}) collective-permute-start(bf16[1,8,64,64]{2,3,1,0:T(8,128)(2,1)S(1)} %copy.75), channel_id=1, source_target_pairs={{0,2},{2,4},{4,6},{1,3},{3,5},{5,7},{8,10},{10,12},{12,14},{9,11},... | collective-permute-start | bytes 196616 | tf_op jit(solution)/shard_map/ppermute | solution.py:16
  15.8 4.9 %collective-permute-start.2 = (bf16[3,1,64,64]{2,3,1,0:T(8,128)(2,1)S(1)}, bf16[3,1,64,64]{2,3,1,0:T(8,128)(2,1)S(1)}, u32[]{:S(2)}, u32[]{:S(2)}) collective-permute-start(bf16[3,1,64,64]{2,3,1,0:T(8,128)(2,1)S(1)} %get-tuple-element.65), channel_id=1, source_target_pairs={{0,1},{2,3},{4,5},{6,7},{8,9},{10,11},{12,13},{14,15},{16,17},{18,... | collective-permute-start | bytes 73736 | tf_op jit(solution)/shard_map/ppermute | solution.py:16
  20.7 18.0 %all_gather.3 = bf16[1,8,64,256]{2,1,0,3:T(8,128)(2,1)S(1)} all-gather(bf16[1,8,64,64]{2,1,0,3:T(8,128)(2,1)S(1)} %copy.104), channel_id=1, replica_groups=mesh['chan'=4,'sx'=4,'sy'=2] {'chan'}, dimensions={3}, use_global_device_ids=true | all-gather | bytes 327680 | tf_op jit(solution)/shard_map/all_gather | solution.py:40
  40.3 3.0 %collective-permute-start.4 = (bf16[1,8,64,256]{3,2,1,0:T(8,128)(2,1)S(1)}, bf16[1,8,64,256]{3,2,1,0:T(8,128)(2,1)S(1)}, u32[]{:S(2)}, u32[]{:S(2)}) collective-permute-start(bf16[1,8,64,256]{3,2,1,0:T(8,128)(2,1)S(1)} %copy.105), channel_id=1, source_target_pairs={{0,2},{2,4},{4,6},{1,3},{3,5},{5,7},{8,10},{10,12},{12,14},{9,11},... | collective-permute-start | bytes 786440 | tf_op jit(solution)/shard_map/ppermute | solution.py:16
  46.0 1.7 fusion.241
  55.4 1.7 reshape.324
  58.7 1.7 reshape.325
  62.0 1.7 reshape.326
  64.4 1.7 reshape.329
  69.0 1.7 reshape.330
  72.3 1.7 reshape.331
  75.6 1.7 reshape.332
  78.0 1.7 reshape.333
  81.3 1.7 reshape.334
  83.0 1.7 copy.90
  84.7 1.7 reshape.335
  87.1 1.7 reshape.337
  90.4 1.7 reshape.338
  92.8 1.7 reshape.339
  100.5 1.7 reshape.343
  103.9 1.7 reshape.344
  140.3 4.6 %collective-permute-start.6 = (bf16[3,1,64,256]{3,2,1,0:T(8,128)(2,1)S(1)}, bf16[3,1,64,256]{3,2,1,0:T(8,128)(2,1)S(1)}, u32[]{:S(2)}, u32[]{:S(2)}) collective-permute-start(bf16[3,1,64,256]{3,2,1,0:T(8,128)(2,1)S(1)} %get-tuple-element.39), channel_id=1, source_target_pairs={{0,1},{2,3},{4,5},{6,7},{8,9},{10,11},{12,13},{14,15},{16,17},{18,... | collective-permute-start | bytes 294920 | tf_op jit(solution)/shard_map/ppermute | solution.py:16
  155.3 34.6 %all-reduce.4.cloned.1.call-done = f32[27,64,256]{2,1,0:T(8,128)} async-done(((f32[27,64,256]{2,1,0:T(8,128)}), f32[27,64,256]{2,1,0:T(8,128)}) %all-reduce.4.cloned.1.call-update) | async-done | bytes 1769488 | tf_op jit(solution)/shard_map/psum | solution.py:62
  189.9 2.9 %broadcast_multiply_fusion = f32[27,64,256]{2,1,0:T(8,128)} fusion(f32[27,64,256]{2,1,0:T(8,128)} %all-reduce.4.cloned.1.call-done), kind=kLoop, calls=%fused_computation.120 | loop fusion | flops 442368 | bytes 3538944 | tf_op jit(solution)/shard_map/div | solution.py:64
  (217 shorter events, 86.4 us)
Async XLA Ops:
  8.0 181.9 %all-reduce.4.cloned.1.call-start = ((), (), s32[]{:S(2)}) async-start(), calls=%async_computation.1 | async-start | bytes 3538944 | tf_op jit(solution)/shard_map/psum | solution.py:62
  9.1 5.4 %collective-permute-start.1 = (bf16[1,8,64,64]{2,3,1,0:T(8,128)(2,1)S(1)}, bf16[1,8,64,64]{2,3,1,0:T(8,128)(2,1)S(1)}, u32[]{:S(2)}, u32[]{:S(2)}) collective-permute-start(bf16[1,8,64,64]{2,3,1,0:T(8,128)(2,1)S(1)} %copy.75), channel_id=1, source_target_pairs={{2,0},{4,2},{6,4},{3,1},{5,3},{7,5},{10,8},{12,10},{14,12},{11,9},... | collective-permute-start | bytes 196616 | tf_op jit(solution)/shard_map/ppermute | solution.py:17
  10.4 4.1 %collective-permute-start = (bf16[1,8,64,64]{2,3,1,0:T(8,128)(2,1)S(1)}, bf16[1,8,64,64]{2,3,1,0:T(8,128)(2,1)S(1)}, u32[]{:S(2)}, u32[]{:S(2)}) collective-permute-start(bf16[1,8,64,64]{2,3,1,0:T(8,128)(2,1)S(1)} %copy.75), channel_id=1, source_target_pairs={{0,2},{2,4},{4,6},{1,3},{3,5},{5,7},{8,10},{10,12},{12,14},{9,11},... | collective-permute-start | bytes 196616 | tf_op jit(solution)/shard_map/ppermute | solution.py:16
  14.5 29.9 %collective-permute-start.3 = (bf16[3,1,64,64]{2,3,1,0:T(8,128)(2,1)S(1)}, bf16[3,1,64,64]{2,3,1,0:T(8,128)(2,1)S(1)}, u32[]{:S(2)}, u32[]{:S(2)}) collective-permute-start(bf16[3,1,64,64]{2,3,1,0:T(8,128)(2,1)S(1)} %get-tuple-element.66), channel_id=1, source_target_pairs={{1,0},{3,2},{5,4},{7,6},{9,8},{11,10},{13,12},{15,14},{17,16},{19,... | collective-permute-start | bytes 73736 | tf_op jit(solution)/shard_map/ppermute | solution.py:17
  15.8 28.7 %collective-permute-start.2 = (bf16[3,1,64,64]{2,3,1,0:T(8,128)(2,1)S(1)}, bf16[3,1,64,64]{2,3,1,0:T(8,128)(2,1)S(1)}, u32[]{:S(2)}, u32[]{:S(2)}) collective-permute-start(bf16[3,1,64,64]{2,3,1,0:T(8,128)(2,1)S(1)} %get-tuple-element.65), channel_id=1, source_target_pairs={{0,1},{2,3},{4,5},{6,7},{8,9},{10,11},{12,13},{14,15},{16,17},{18,... | collective-permute-start | bytes 73736 | tf_op jit(solution)/shard_map/ppermute | solution.py:16
  39.0 99.3 %collective-permute-start.5 = (bf16[1,8,64,256]{3,2,1,0:T(8,128)(2,1)S(1)}, bf16[1,8,64,256]{3,2,1,0:T(8,128)(2,1)S(1)}, u32[]{:S(2)}, u32[]{:S(2)}) collective-permute-start(bf16[1,8,64,256]{3,2,1,0:T(8,128)(2,1)S(1)} %copy.105), channel_id=1, source_target_pairs={{2,0},{4,2},{6,4},{3,1},{5,3},{7,5},{10,8},{12,10},{14,12},{11,9},... | collective-permute-start | bytes 786440 | tf_op jit(solution)/shard_map/ppermute | solution.py:17
  40.3 98.0 %collective-permute-start.4 = (bf16[1,8,64,256]{3,2,1,0:T(8,128)(2,1)S(1)}, bf16[1,8,64,256]{3,2,1,0:T(8,128)(2,1)S(1)}, u32[]{:S(2)}, u32[]{:S(2)}) collective-permute-start(bf16[1,8,64,256]{3,2,1,0:T(8,128)(2,1)S(1)} %copy.105), channel_id=1, source_target_pairs={{0,2},{2,4},{4,6},{1,3},{3,5},{5,7},{8,10},{10,12},{12,14},{9,11},... | collective-permute-start | bytes 786440 | tf_op jit(solution)/shard_map/ppermute | solution.py:16
  46.0 3.7 %copy-start = (bf16[27,64,256]{2,1,0:T(8,128)(2,1)S(1)}, bf16[27,64,256]{2,1,0:T(8,128)(2,1)}, u32[]{:S(2)}) copy-start(bf16[27,64,256]{2,1,0:T(8,128)(2,1)} %param.4) | copy-start | bytes 2654212
  67.6 24.5 %copy-start.6 = (bf16[1,8,64,64]{2,3,1,0:T(8,128)(2,1)}, bf16[1,8,64,64]{2,3,1,0:T(8,128)(2,1)S(1)}, u32[]{:S(2)}) copy-start(bf16[1,8,64,64]{2,3,1,0:T(8,128)(2,1)S(1)} %get-tuple-element.61) | copy-start | bytes 196612
  67.6 18.8 %copy-start.14 = (bf16[1,8,64,64]{2,3,1,0:T(8,128)(2,1)S(1)}, bf16[1,8,64,64]{2,3,1,0:T(8,128)(2,1)}, u32[]{:S(2)}) copy-start(bf16[1,8,64,64]{2,3,1,0:T(8,128)(2,1)} %get-tuple-element.49) | copy-start | bytes 196612
  87.1 18.5 %copy-start.9 = (bf16[1,8,64,64]{2,3,1,0:T(8,128)(2,1)S(1)}, bf16[1,8,64,64]{2,3,1,0:T(8,128)(2,1)}, u32[]{:S(2)}) copy-start(bf16[1,8,64,64]{2,3,1,0:T(8,128)(2,1)} %copy-done.8) | copy-start | bytes 196612
  100.5 10.2 %copy-start.11 = (bf16[1,8,64,64]{2,3,1,0:T(8,128)(2,1)S(1)}, bf16[1,8,64,64]{2,3,1,0:T(8,128)(2,1)}, u32[]{:S(2)}) copy-start(bf16[1,8,64,64]{2,3,1,0:T(8,128)(2,1)} %copy-done.10) | copy-start | bytes 196612
  109.0 7.0 %copy-start.3 = (bf16[1,8,64,64]{3,2,1,0:T(8,128)(2,1)S(1)}, bf16[1,8,64,64]{3,2,1,0:T(8,128)(2,1)}, u32[]{:S(2)}) copy-start(bf16[1,8,64,64]{3,2,1,0:T(8,128)(2,1)} %param.3) | copy-start | bytes 196612
  111.6 7.0 %copy-start.7 = (bf16[1,8,64,64]{2,3,1,0:T(8,128)(2,1)S(1)}, bf16[1,8,64,64]{2,3,1,0:T(8,128)(2,1)}, u32[]{:S(2)}) copy-start(bf16[1,8,64,64]{2,3,1,0:T(8,128)(2,1)} %copy-done.6) | copy-start | bytes 196612
  119.4 7.0 %copy-start.4 = (bf16[1,8,64,64]{2,3,1,0:T(8,128)(2,1)S(1)}, bf16[1,8,64,64]{2,3,1,0:T(8,128)(2,1)}, u32[]{:S(2)}) copy-start(bf16[1,8,64,64]{2,3,1,0:T(8,128)(2,1)} %get-tuple-element.59) | copy-start | bytes 196612
  124.6 3.8 %copy-start.2 = (f32[512,256]{1,0:T(8,128)S(1)}, f32[512,256]{1,0:T(8,128)}, u32[]{:S(2)}) copy-start(f32[512,256]{1,0:T(8,128)} %fusion.166) | copy-start | bytes 1572868
  128.2 3.7 %copy-start.15 = (bf16[512,64]{0,1:T(8,128)(2,1)S(1)}, bf16[512,64]{0,1:T(8,128)(2,1)}, u32[]{:S(2)}) copy-start(bf16[512,64]{0,1:T(8,128)(2,1)} %reshape.327) | copy-start | bytes 196612
  128.2 64.6 %reduce-scatter.4.cloned.1.call-start = ((), (), s32[]{:S(2)}) async-start(), calls=%async_computation.2 | async-start | bytes 655360
  128.4 3.4 %copy-start.1 = (f32[512,256]{1,0:T(8,128)S(1)}, f32[512,256]{1,0:T(8,128)}, u32[]{:S(2)}) copy-start(f32[512,256]{1,0:T(8,128)} %fusion.154) | copy-start | bytes 1572868
  129.6 2.6 %copy-start.16 = (bf16[512,64]{0,1:T(8,128)(2,1)S(1)}, bf16[512,64]{0,1:T(8,128)(2,1)}, u32[]{:S(2)}) copy-start(bf16[512,64]{0,1:T(8,128)(2,1)} %reshape.329) | copy-start | bytes 196612
  130.7 1.7 copy-start.17
  136.7 1.1 copy-start.12
  139.0 7.6 %collective-permute-start.7 = (bf16[3,1,64,256]{3,2,1,0:T(8,128)(2,1)}, bf16[3,1,64,256]{3,2,1,0:T(8,128)(2,1)S(1)}, u32[]{:S(2)}, u32[]{:S(2)}) collective-permute-start(bf16[3,1,64,256]{3,2,1,0:T(8,128)(2,1)} %get-tuple-element.40), channel_id=1, source_target_pairs={{1,0},{3,2},{5,4},{7,6},{9,8},{11,10},{13,12},{15,14},{17,16},{19,... | collective-permute-start | bytes 294920 | tf_op jit(solution)/shard_map/ppermute | solution.py:17
  140.3 6.8 %collective-permute-start.6 = (bf16[3,1,64,256]{3,2,1,0:T(8,128)(2,1)S(1)}, bf16[3,1,64,256]{3,2,1,0:T(8,128)(2,1)S(1)}, u32[]{:S(2)}, u32[]{:S(2)}) collective-permute-start(bf16[3,1,64,256]{3,2,1,0:T(8,128)(2,1)S(1)} %get-tuple-element.39), channel_id=1, source_target_pairs={{0,1},{2,3},{4,5},{6,7},{8,9},{10,11},{12,13},{14,15},{16,17},{18,... | collective-permute-start | bytes 294920 | tf_op jit(solution)/shard_map/ppermute | solution.py:16
  (19 other events, 15.5 us)
Sparse Core Ops, SparseCore 0:
  128.3 61.5 all-reduce.3
Sparse Core Ops, SparseCore 1:
  146.7 22.8 reduce-scatter.3
where the time goes:
time: 203 us; the launch traced here: 202 us
  local copies, waits for them, and re-layouts  64.2 us (32%)
  matrix products  40.7 us (20%)
  waiting for transfers between devices  35 us (17%)
  starting transfers between devices  20.9 us (10%)
  blocking collectives  18 us (9%)
  between operations  16.1 us (8%)
  other arithmetic  7.05 us (3%)
    psum x1, waiting for transfers between devices, body(): summed = lax.psum(local_kernel, ('sx', 'sy'))  34.6 us
    reshape x26, local copies, waits for them, and re-layouts, body(): padded[a:a + size_x, b:b + size_y, e:e + size_z].reshape(cells, own_in)  29.9 us
    slice x25, local copies, waits for them, and re-layouts, body(): padded[a:a + size_x, b:b + size_y, e:e + size_z].reshape(cells, own_in)  23.6 us
    dot_general x27, matrix products, body(): lax.dot_general(in_window, flat_grad, (((0,), (0,)), ((), ())), preferred...  23.4 us
    all_gather x1, blocking collectives, body(): grad_full = lax.all_gather(grad_out, 'chan', axis=3, tiled=True)  18 us
    ppermute x4, starting transfers between devices, padded_2(): before = lax.ppermute(last, axis, up)  15.5 us
    dot_general x27, matrix products, body(): jnp.dot(window, kernel[index], preferred_element_type=jnp.float32)  11.7 us
    unnamed x73, local copies, waits for them, and re-layouts  9.34 us
  transfers between devices with their start and end apart: 10, of which 2 were waited for; matrix products, arithmetic and copies ran while one was open for 52% of the time, Pallas kernels for 0%

commit v1 on v0

--- a/solution.py
+++ b/solution.py
@@ -1,8 +1,11 @@
+import functools
 import math
 
 import jax
 import jax.numpy as jnp
 from jax import lax
+from jax.experimental import pallas as pl
+from jax.experimental.pallas import tpu as pltpu
 from jax.sharding import PartitionSpec as P
 
 
@@ -65,9 +68,258 @@
     return (out, grad_input, grad_kernel)
 
 
+MESH = pl.DeviceIdType.MESH
+F32 = jnp.float32
+BF16 = jnp.bfloat16
+
+
+def fused_kernel(
+    vol_ref, w_ref, g_ref, out_ref, gi_ref, gk_ref,
+    blocks, gpad, v3, vt, part, got, z_send, z_recv, p_send, p_recv, r_send, r_recv,
+    *, scale,
+):
+    chans, count_s, count_h = lax.axis_size("chan"), lax.axis_size("sx"), lax.axis_size("sy")
+    c, s, h = lax.axis_index("chan"), lax.axis_index("sx"), lax.axis_index("sy")
+    rows_y, size_z, ch = vol_ref.shape[1:]
+    half = rows_y // 2
+    cells = half * size_z
+    total = w_ref.shape[2]
+    wide = 3 * ch
+    core, far_s, far_h = s + 1 - 2 * (s % 2), (s + 2) % 4, 1 - h
+    others = (c + 1 - 2 * (c % 2), (c + 2) % 4, 3 - c)
+    to_x, to_y, to_core = {"sx": far_s}, {"sy": far_h}, {"sx": core}
+    sent = []
+
+    def remote(src, dst, send, recv, where):
+        return pltpu.make_async_remote_copy(
+            src_ref=src, dst_ref=dst, send_sem=send, recv_sem=recv,
+            device_id=where, device_id_type=MESH,
+        )
+
+    def push(src, send, recv, where, dst=None):
+        copy = remote(src, src if dst is None else dst, send, recv, where)
+        copy.start()
+        sent.append(copy)
+
+    def arrived(ref, send, recv, where):
+        remote(ref, ref, send, recv, where).wait_recv()
+
+    for index, ref in ((c, g_ref), (chans, vol_ref)):
+        blocks[index, s, h, :, :, :ch] = ref[0, :half]
+        blocks[index, s, h, :, :, ch:] = ref[0, half:]
+
+    barrier = pltpu.get_barrier_semaphore()
+    partners = [{"chan": d} for d in others] + [to_x, to_y, to_core]
+    for where in partners:
+        pl.semaphore_signal(barrier, inc=1, device_id=where, device_id_type=MESH)
+    pl.semaphore_wait(barrier, len(partners))
+
+    def offer(k, index):
+        own = blocks.at[index, s, h]
+        push(own, p_send.at[k, 0], p_recv.at[k, 0], to_x)
+        push(own, p_send.at[k, 1], p_recv.at[k, 1], to_y)
+        push(own, p_send.at[k, 2], p_recv.at[k, 2], to_core)
+
+    def relay(k, index):
+        from_x, from_y = blocks.at[index, far_s, h], blocks.at[index, s, far_h]
+        cut = half // 2
+        arrived(from_x, p_send.at[k, 0], p_recv.at[k, 0], to_x)
+        push(from_x.at[:cut], p_send.at[k, 3], p_recv.at[k, 3], to_y)
+        push(from_x, p_send.at[k, 5], p_recv.at[k, 5], to_core)
+        arrived(from_y, p_send.at[k, 1], p_recv.at[k, 1], to_y)
+        push(from_y.at[cut:], p_send.at[k, 4], p_recv.at[k, 4], to_x)
+        push(from_y, p_send.at[k, 6], p_recv.at[k, 6], to_core)
+
+    def corner(k, index):
+        diag = blocks.at[index, far_s, far_h]
+        cut = half // 2
+        arrived(diag.at[:cut], p_send.at[k, 3], p_recv.at[k, 3], to_y)
+        arrived(diag.at[cut:], p_send.at[k, 4], p_recv.at[k, 4], to_x)
+        push(diag, p_send.at[k, 7], p_recv.at[k, 7], to_core)
+
+    def from_core(k, index):
+        far_core = 3 - s
+        arrived(blocks.at[index, core, h], p_send.at[k, 2], p_recv.at[k, 2], to_core)
+        arrived(blocks.at[index, far_core, h], p_send.at[k, 5], p_recv.at[k, 5], to_core)
+        arrived(blocks.at[index, core, far_h], p_send.at[k, 6], p_recv.at[k, 6], to_core)
+        arrived(blocks.at[index, far_core, far_h], p_send.at[k, 7], p_recv.at[k, 7], to_core)
+
+    def from_chan(j):
+        index = others[j]
+        arrived(blocks.at[index, s, h], z_send.at[j], z_recv.at[j], {"chan": index})
+        offer(j + 2, index)
+
+    offer(0, chans)
+    for j, d in enumerate(others):
+        push(blocks.at[c, s, h], z_send.at[j], z_recv.at[j], {"chan": d})
+    offer(1, c)
+
+    zero_row = jnp.zeros((size_z, total), BF16)
+    zero_v = jnp.zeros((size_z, wide), BF16)
+    last_x, last_y = gpad.shape[0] - 1, gpad.shape[1] - 1
+
+    @pl.loop(0, gpad.shape[1])
+    def _(y):
+        for x in (0, last_x):
+            gpad[x, y] = zero_row
+            v3[x, y] = zero_v
+
+    for x in range(1, last_x):
+        for y in (0, last_y):
+            gpad[x, y] = zero_row
+            v3[x, y] = zero_v
+
+    relay(0, chans)
+    corner(0, chans)
+    from_chan(0)
+    relay(1, c)
+    from_core(0, chans)
+
+    row = lax.broadcasted_iota(jnp.int32, (cells, 2 * ch), 0) % size_z
+
+    def spread(x, hy):
+        centre = blocks[chans, x, hy].reshape(cells, 2 * ch)
+        wide_centre = centre.astype(F32)
+        before = jnp.where(row == 0, 0.0, pltpu.roll(wide_centre, 1, 0))
+        after = jnp.where(row == size_z - 1, 0.0, pltpu.roll(wide_centre, cells - 1, 0))
+        for e, moved in enumerate((before, wide_centre, after)):
+            narrow = moved.astype(BF16).reshape(half, size_z, 2 * ch)
+            turned = moved.T.astype(BF16)
+            for k in range(2):
+                v3[x + 1, pl.ds(1 + hy * rows_y + k * half, half), :, e * ch : (e + 1) * ch] = (
+                    narrow[:, :, k * ch : (k + 1) * ch]
+                )
+                vt[x, hy * 2 + k, e * ch : (e + 1) * ch, :] = turned[k * ch : (k + 1) * ch]
+
+    @pl.loop(0, count_s * count_h)
+    def _(n):
+        spread(n // count_h, n % count_h)
+
+    corner(1, c)
+    relay(2, others[0])
+    from_chan(1)
+
+    @pl.loop(0, 2)
+    def _(t):
+        acc = jnp.zeros((cells, total), F32)
+        for a in range(3):
+            for b in range(3):
+                window = v3[s + a, pl.ds(h * rows_y + t * half + b, half)].reshape(cells, wide)
+                acc = acc + jnp.dot(window, w_ref[3 * a + b], preferred_element_type=F32)
+        part[t] = acc
+
+    for d in range(chans):
+        for k in range(2):
+            got[chans + d, :, k * ch : (k + 1) * ch] = part[k, :, d * ch : (d + 1) * ch]
+
+    for j, d in enumerate(others):
+        push(got.at[chans + d], r_send.at[j], r_recv.at[j], {"chan": d}, dst=got.at[c])
+
+    corner(2, others[0])
+    relay(3, others[1])
+    from_chan(2)
+    corner(3, others[1])
+    relay(4, others[2])
+    corner(4, others[2])
+    for k, index in enumerate((c,) + others):
+        from_core(k + 1, index)
+
+    @pl.loop(0, count_s * count_h)
+    def _(n):
+        x, hy = n // count_h, n % count_h
+        for d in range(chans):
+            for k in range(2):
+                gpad[x + 1, pl.ds(1 + hy * rows_y + k * half, half), :, d * ch : (d + 1) * ch] = (
+                    blocks[d, x, hy, :, :, k * ch : (k + 1) * ch]
+                )
+
+    row_out = lax.broadcasted_iota(jnp.int32, (cells, ch), 0) % size_z
+
+    @pl.loop(0, 2)
+    def _(t):
+        acc = jnp.zeros((cells, wide), F32)
+        for a in range(3):
+            for b in range(3):
+                window = gpad[s + 2 - a, pl.ds(h * rows_y + t * half + 2 - b, half)]
+                acc = acc + lax.dot_general(
+                    window.reshape(cells, total), w_ref[3 * a + b],
+                    (((1,), (1,)), ((), ())), preferred_element_type=F32,
+                )
+        first, middle, final = acc[:, :ch], acc[:, ch : 2 * ch], acc[:, 2 * ch :]
+        later = jnp.where(row_out == size_z - 1, 0.0, pltpu.roll(first, cells - 1, 0))
+        sooner = jnp.where(row_out == 0, 0.0, pltpu.roll(final, 1, 0))
+        gi_ref[0, pl.ds(t * half, half)] = (
+            (later + middle + sooner).astype(BF16).reshape(half, size_z, ch)
+        )
+
+    for a in range(3):
+
+        @pl.loop(0, 3)
+        def _(b):
+            acc = jnp.zeros((wide, total), F32)
+            for x in range(count_s):
+                if 0 <= x + 1 - a < count_s:
+                    for t in range(2 * count_h):
+                        rows = gpad[x + 2 - a, pl.ds(2 - b + t * half, half)]
+                        acc = acc + jnp.dot(
+                            vt[x, t], rows.reshape(cells, total), preferred_element_type=F32
+                        )
+            gk_ref[3 * a + b] = acc / scale
+
+    for j, d in enumerate(others):
+        arrived(got.at[d], r_send.at[j], r_recv.at[j], {"chan": d})
+    summed = got[chans + c]
+    for d in others:
+        summed = summed + got[d]
+    narrow = summed.astype(BF16).reshape(half, size_z, 2 * ch)
+    out_ref[0, :half] = narrow[:, :, :ch]
+    out_ref[0, half:] = narrow[:, :, ch:]
+    for copy in sent:
+        copy.wait_send()
+
+
+def fused_body(volume, kernel, grad_out):
+    chans, count_s, count_h = lax.axis_size("chan"), lax.axis_size("sx"), lax.axis_size("sy")
+    _, rows_y, size_z, ch = volume.shape
+    total = kernel.shape[2]
+    half, wide = rows_y // 2, 3 * ch
+    cells = half * size_z
+    all_y = rows_y * count_h
+    scale = math.sqrt(count_s * all_y * size_z)
+    weights = kernel.reshape(9, wide, total)
+    vmem = pl.BlockSpec(memory_space=pltpu.VMEM)
+    dma = pltpu.SemaphoreType.DMA
+    out, gi, gk = pl.pallas_call(
+        functools.partial(fused_kernel, scale=scale),
+        out_shape=(
+            jax.ShapeDtypeStruct(volume.shape, BF16),
+            jax.ShapeDtypeStruct(volume.shape, BF16),
+            jax.ShapeDtypeStruct(weights.shape, F32),
+        ),
+        in_specs=[vmem] * 3,
+        out_specs=(vmem,) * 3,
+        scratch_shapes=[
+            pltpu.VMEM((chans + 1, count_s, count_h, half, size_z, 2 * ch), BF16),
+            pltpu.VMEM((count_s + 2, all_y + 2, size_z, total), BF16),
+            pltpu.VMEM((count_s + 2, all_y + 2, size_z, wide), BF16),
+            pltpu.VMEM((count_s, 2 * count_h, wide, cells), BF16),
+            pltpu.VMEM((2, cells, total), F32),
+            pltpu.VMEM((2 * chans, cells, 2 * ch), F32),
+            dma((chans - 1,)), dma((chans - 1,)),
+            dma((chans + 1, 8)), dma((chans + 1, 8)),
+            dma((chans - 1,)), dma((chans - 1,)),
+        ],
+        compiler_params=pltpu.CompilerParams(
+            collective_id=0, has_side_effects=True, vmem_limit_bytes=50 * 2**20
+        ),
+    )(volume, weights, grad_out)
+    return out, gi, gk.reshape(kernel.shape)
+
+
 def solution(mesh):
+    small = (mesh.shape["chan"], mesh.shape["sx"], mesh.shape["sy"]) == (4, 4, 2)
     return jax.shard_map(
-        body,
+        fused_body if small else body,
         mesh=mesh,
         in_specs=(P("sx", "sy", None, "chan"), P(None, "chan", None), P("sx", "sy", None, "chan")),
         out_specs=(P("sx", "sy", None, "chan"), P("sx", "sy", None, "chan"), P(None, "chan", None)),

time: 203 us -> 42.4 us (0.21)
  the two profiles are of different devices: /device:TPU:0 before, /device:TPU:1 now
where the time goes in v1:
time: 42.4 us; the launch traced here: 42.2 us
  Pallas kernels  36.1 us (85%)
  local copies, waits for them, and re-layouts  5.49 us (13%)
  between operations  0.65 us (2%)
    pallas_call x1, Pallas kernels, fused_body(): pl.pallas_call(functools.partial(fused_kernel, scale=scale), out_shape=(j...  36.1 us
    unnamed x9, local copies, waits for them, and re-layouts  5.49 us

profile of v1, /device:TPU:1, one launch (start us, length us, event | category | flops | bytes accessed | tf_op | source)
XLA Modules:
  0.0 42.2 jit_solution(49616294028150799)
XLA Ops:
  0.6 0.0 copy-start
  0.6 1.2 %copy-done = bf16[27,64,256]{2,1,0:T(8,128)(2,1)S(1)} copy-done((bf16[27,64,256]{2,1,0:T(8,128)(2,1)S(1)}, bf16[27,64,256]{2,1,0:T(8,128)(2,1)}, u32[]{:S(2)}) %copy-start) | copy-done | bytes 884760
  1.8 0.0 copy-start.1
  1.8 0.9 %copy-done.1 = bf16[1,8,64,64]{3,2,1,0:T(8,128)(2,1)S(1)} copy-done((bf16[1,8,64,64]{3,2,1,0:T(8,128)(2,1)S(1)}, bf16[1,8,64,64]{3,2,1,0:T(8,128)(2,1)}, u32[]{:S(2)}) %copy-start.1) | copy-done | bytes 65560
  2.7 0.0 copy-start.2
  2.7 0.9 %copy-done.2 = bf16[1,8,64,64]{3,2,1,0:T(8,128)(2,1)S(1)} copy-done((bf16[1,8,64,64]{3,2,1,0:T(8,128)(2,1)S(1)}, bf16[1,8,64,64]{3,2,1,0:T(8,128)(2,1)}, u32[]{:S(2)}) %copy-start.2) | copy-done | bytes 65560
  3.6 36.1 %shard_map.58 = (bf16[1,8,64,64]{3,2,1,0:T(8,128)(2,1)S(1)}, bf16[1,8,64,64]{3,2,1,0:T(8,128)(2,1)S(1)}, f32[9,192,256]{2,1,0:T(8,128)S(1)}) custom-call(bf16[1,8,64,64]{3,2,1,0:T(8,128)(2,1)S(1)} %copy-done.1, bf16[9,192,256]{2,1,0:T(8,128)(2,1)S(1)} %bitcast.3, bf16[1,8,64,64]{3,2,1,0:T(8,128)(2,1)S(1)} %copy-done.2), custom_call_target="tpu_custom_call" | custom-call | tf_op jit(solution)/shard_map/pallas_call | solution.py:292
  39.7 0.7 %copy.9 = bf16[1,8,64,64]{3,2,1,0:T(8,128)(2,1)} copy(bf16[1,8,64,64]{3,2,1,0:T(8,128)(2,1)S(1)} %get-tuple-element.12) | data formatting | bytes 131072
  40.3 0.7 %copy.10 = bf16[1,8,64,64]{3,2,1,0:T(8,128)(2,1)} copy(bf16[1,8,64,64]{3,2,1,0:T(8,128)(2,1)S(1)} %get-tuple-element.13) | data formatting | bytes 131072
  41.0 1.2 %copy.11 = f32[27,64,256]{2,1,0:T(8,128)} copy(f32[27,64,256]{2,1,0:T(8,128)S(1)} %bitcast.2) | data formatting | bytes 3538944
Async XLA Ops:
  0.6 1.2 %copy-start = (bf16[27,64,256]{2,1,0:T(8,128)(2,1)S(1)}, bf16[27,64,256]{2,1,0:T(8,128)(2,1)}, u32[]{:S(2)}) copy-start(bf16[27,64,256]{2,1,0:T(8,128)(2,1)} %param.4) | copy-start | bytes 2654212
  1.8 0.9 %copy-start.1 = (bf16[1,8,64,64]{3,2,1,0:T(8,128)(2,1)S(1)}, bf16[1,8,64,64]{3,2,1,0:T(8,128)(2,1)}, u32[]{:S(2)}) copy-start(bf16[1,8,64,64]{3,2,1,0:T(8,128)(2,1)} %vol_ref.1) | copy-start | bytes 196612
  2.7 0.9 %copy-start.2 = (bf16[1,8,64,64]{3,2,1,0:T(8,128)(2,1)S(1)}, bf16[1,8,64,64]{3,2,1,0:T(8,128)(2,1)}, u32[]{:S(2)}) copy-start(bf16[1,8,64,64]{3,2,1,0:T(8,128)(2,1)} %g_ref.1) | copy-start | bytes 196612

commit v2 on v1

--- a/solution.py
+++ b/solution.py
@@ -74,8 +74,9 @@
 
 
 def fused_kernel(
-    vol_ref, w_ref, g_ref, out_ref, gi_ref, gk_ref,
-    blocks, gpad, v3, vt, part, got, z_send, z_recv, p_send, p_recv, r_send, r_recv,
+    vol_hbm, w_hbm, g_hbm, out_ref, gi_ref, gk_ref,
+    vol_ref, w_ref, g_ref, blocks, gpad, v3, vt, part, got,
+    in_sem, z_send, z_recv, p_send, p_recv, r_send, r_recv, k_send, k_recv,
     *, scale,
 ):
     chans, count_s, count_h = lax.axis_size("chan"), lax.axis_size("sx"), lax.axis_size("sy")
@@ -104,14 +105,38 @@
     def arrived(ref, send, recv, where):
         remote(ref, ref, send, recv, where).wait_recv()
 
-    for index, ref in ((c, g_ref), (chans, vol_ref)):
-        blocks[index, s, h, :, :, :ch] = ref[0, :half]
-        blocks[index, s, h, :, :, ch:] = ref[0, half:]
-
+    loads = [
+        pltpu.make_async_copy(src, dst, in_sem.at[k])
+        for k, (src, dst) in enumerate(((g_hbm, g_ref), (vol_hbm, vol_ref), (w_hbm, w_ref)))
+    ]
+    for load in loads:
+        load.start()
     barrier = pltpu.get_barrier_semaphore()
     partners = [{"chan": d} for d in others] + [to_x, to_y, to_core]
     for where in partners:
         pl.semaphore_signal(barrier, inc=1, device_id=where, device_id_type=MESH)
+
+    zero_row = jnp.zeros((2, size_z, total // 2), BF16)
+    zero_v = jnp.zeros((size_z, wide), BF16)
+    last_x, last_y = v3.shape[0] - 1, v3.shape[1] - 1
+
+    @pl.loop(0, last_y + 1)
+    def _(y):
+        for x in (0, last_x):
+            gpad[:, x, y] = zero_row
+            v3[x, y] = zero_v
+
+    for x in range(1, last_x):
+        for y in (0, last_y):
+            gpad[:, x, y] = zero_row
+            v3[x, y] = zero_v
+
+    loads[0].wait()
+    loads[1].wait()
+    for index, ref in ((c, g_ref), (chans, vol_ref)):
+        blocks[index, s, h, :, :, :ch] = ref[0, :half]
+        blocks[index, s, h, :, :, ch:] = ref[0, half:]
+
     pl.semaphore_wait(barrier, len(partners))
 
     def offer(k, index):
@@ -154,53 +179,38 @@
         push(blocks.at[c, s, h], z_send.at[j], z_recv.at[j], {"chan": d})
     offer(1, c)
 
-    zero_row = jnp.zeros((size_z, total), BF16)
-    zero_v = jnp.zeros((size_z, wide), BF16)
-    last_x, last_y = gpad.shape[0] - 1, gpad.shape[1] - 1
-
-    @pl.loop(0, gpad.shape[1])
-    def _(y):
-        for x in (0, last_x):
-            gpad[x, y] = zero_row
-            v3[x, y] = zero_v
-
-    for x in range(1, last_x):
-        for y in (0, last_y):
-            gpad[x, y] = zero_row
-            v3[x, y] = zero_v
-
     relay(0, chans)
+    relay(1, c)
     corner(0, chans)
     from_chan(0)
-    relay(1, c)
+    corner(1, c)
     from_core(0, chans)
+    relay(2, others[0])
+    from_chan(1)
 
     row = lax.broadcasted_iota(jnp.int32, (cells, 2 * ch), 0) % size_z
 
-    def spread(x, hy):
-        centre = blocks[chans, x, hy].reshape(cells, 2 * ch)
-        wide_centre = centre.astype(F32)
-        before = jnp.where(row == 0, 0.0, pltpu.roll(wide_centre, 1, 0))
-        after = jnp.where(row == size_z - 1, 0.0, pltpu.roll(wide_centre, cells - 1, 0))
-        for e, moved in enumerate((before, wide_centre, after)):
-            narrow = moved.astype(BF16).reshape(half, size_z, 2 * ch)
-            turned = moved.T.astype(BF16)
-            for k in range(2):
-                v3[x + 1, pl.ds(1 + hy * rows_y + k * half, half), :, e * ch : (e + 1) * ch] = (
-                    narrow[:, :, k * ch : (k + 1) * ch]
-                )
-                vt[x, hy * 2 + k, e * ch : (e + 1) * ch, :] = turned[k * ch : (k + 1) * ch]
+    def shifted(x, hy):
+        centre = blocks[chans, x, hy].reshape(cells, 2 * ch).astype(F32)
+        before = jnp.where(row == 0, 0.0, pltpu.roll(centre, 1, 0))
+        after = jnp.where(row == size_z - 1, 0.0, pltpu.roll(centre, cells - 1, 0))
+        return before.astype(BF16), centre.astype(BF16), after.astype(BF16)
 
     @pl.loop(0, count_s * count_h)
     def _(n):
-        spread(n // count_h, n % count_h)
-
-    corner(1, c)
-    relay(2, others[0])
-    from_chan(1)
-
-    @pl.loop(0, 2)
-    def _(t):
+        x, hy = n // count_h, n % count_h
+        parts = [moved.reshape(half, size_z, 2 * ch) for moved in shifted(x, hy)]
+        for k in range(2):
+            v3[x + 1, pl.ds(1 + hy * rows_y + k * half, half)] = jnp.concatenate(
+                [moved[:, :, k * ch : (k + 1) * ch] for moved in parts], axis=-1
+            )
+
+    corner(2, others[0])
+    relay(3, others[1])
+    from_chan(2)
+    loads[2].wait()
+
+    for t in range(2):
         acc = jnp.zeros((cells, total), F32)
         for a in range(3):
             for b in range(3):
@@ -215,34 +225,78 @@
     for j, d in enumerate(others):
         push(got.at[chans + d], r_send.at[j], r_recv.at[j], {"chan": d}, dst=got.at[c])
 
-    corner(2, others[0])
-    relay(3, others[1])
-    from_chan(2)
     corner(3, others[1])
     relay(4, others[2])
-    corner(4, others[2])
-    for k, index in enumerate((c,) + others):
-        from_core(k + 1, index)
 
     @pl.loop(0, count_s * count_h)
     def _(n):
         x, hy = n // count_h, n % count_h
-        for d in range(chans):
+        for e, moved in enumerate(shifted(x, hy)):
+            turned = moved.T
             for k in range(2):
-                gpad[x + 1, pl.ds(1 + hy * rows_y + k * half, half), :, d * ch : (d + 1) * ch] = (
-                    blocks[d, x, hy, :, :, k * ch : (k + 1) * ch]
+                at = pl.multiple_of((hy * 2 + k) * cells, cells)
+                vt[x, e * ch : (e + 1) * ch, pl.ds(at, cells)] = turned[k * ch : (k + 1) * ch]
+
+    corner(4, others[2])
+
+    def fill(pair):
+        @pl.loop(0, count_s * count_h)
+        def _(n):
+            x, hy = n // count_h, n % count_h
+            one, two = blocks[2 * pair, x, hy], blocks[2 * pair + 1, x, hy]
+            for k in range(2):
+                lanes = slice(k * ch, (k + 1) * ch)
+                gpad[pair, x + 1, pl.ds(1 + hy * rows_y + k * half, half)] = jnp.concatenate(
+                    [one[:, :, lanes], two[:, :, lanes]], axis=-1
                 )
 
+    from_core(1, c)
+    from_core(2, others[0])
+    fill(c // 2)
+    from_core(3, others[1])
+    from_core(4, others[2])
+    fill(1 - c // 2)
+
+    def cotangent(x, start, rows):
+        return jnp.concatenate(
+            [gpad[p, x, pl.ds(start, rows)].reshape(rows * size_z, total // 2) for p in range(2)],
+            axis=-1,
+        )
+
+    core_at = s % 2
+    all_y = rows_y * count_h
+    top = wide // 2
+
+    def weight_gradient(step, index, terms, at, rows):
+        acc = jnp.zeros((rows, total), F32)
+        for x_in, x_out, start in terms:
+            acc = acc + jnp.dot(
+                vt[x_in, pl.ds(at, rows), :], cotangent(x_out, start, all_y),
+                preferred_element_type=F32,
+            )
+        gk_ref[index, pl.ds(at, rows)] = acc / scale
+        push(gk_ref.at[index, pl.ds(at, rows)], k_send.at[step], k_recv.at[step], to_core)
+
+    for b in range(3):
+        weight_gradient(
+            b, 6 * core_at + b,
+            [(x + core_at, x + 2 - core_at, 2 - b) for x in range(count_s - 1)], 0, wide,
+        )
+    weight_gradient(
+        3, 3 + 2 * core_at, [(x, x + 1, 2 - 2 * core_at) for x in range(count_s)], 0, wide
+    )
+    weight_gradient(
+        4, 4, [(x, x + 1, 1) for x in range(count_s)], pl.multiple_of(core_at * top, top), top
+    )
+
     row_out = lax.broadcasted_iota(jnp.int32, (cells, ch), 0) % size_z
-
-    @pl.loop(0, 2)
-    def _(t):
+    for t in range(2):
         acc = jnp.zeros((cells, wide), F32)
         for a in range(3):
             for b in range(3):
-                window = gpad[s + 2 - a, pl.ds(h * rows_y + t * half + 2 - b, half)]
+                window = cotangent(s + 2 - a, h * rows_y + t * half + 2 - b, half)
                 acc = acc + lax.dot_general(
-                    window.reshape(cells, total), w_ref[3 * a + b],
+                    window, w_ref[3 * a + b],
                     (((1,), (1,)), ((), ())), preferred_element_type=F32,
                 )
         first, middle, final = acc[:, :ch], acc[:, ch : 2 * ch], acc[:, 2 * ch :]
@@ -251,20 +305,6 @@
         gi_ref[0, pl.ds(t * half, half)] = (
             (later + middle + sooner).astype(BF16).reshape(half, size_z, ch)
         )
-
-    for a in range(3):
-
-        @pl.loop(0, 3)
-        def _(b):
-            acc = jnp.zeros((wide, total), F32)
-            for x in range(count_s):
-                if 0 <= x + 1 - a < count_s:
-                    for t in range(2 * count_h):
-                        rows = gpad[x + 2 - a, pl.ds(2 - b + t * half, half)]
-                        acc = acc + jnp.dot(
-                            vt[x, t], rows.reshape(cells, total), preferred_element_type=F32
-                        )
-            gk_ref[3 * a + b] = acc / scale
 
     for j, d in enumerate(others):
         arrived(got.at[d], r_send.at[j], r_recv.at[j], {"chan": d})
@@ -274,6 +314,12 @@
     narrow = summed.astype(BF16).reshape(half, size_z, 2 * ch)
     out_ref[0, :half] = narrow[:, :, :ch]
     out_ref[0, half:] = narrow[:, :, ch:]
+
+    for b in range(3):
+        arrived(gk_ref.at[6 * (1 - core_at) + b], k_send.at[b], k_recv.at[b], to_core)
+    arrived(gk_ref.at[5 - 2 * core_at], k_send.at[3], k_recv.at[3], to_core)
+    below = pl.multiple_of((1 - core_at) * top, top)
+    arrived(gk_ref.at[4, pl.ds(below, top)], k_send.at[4], k_recv.at[4], to_core)
     for copy in sent:
         copy.wait_send()
 
@@ -296,18 +342,23 @@
             jax.ShapeDtypeStruct(volume.shape, BF16),
             jax.ShapeDtypeStruct(weights.shape, F32),
         ),
-        in_specs=[vmem] * 3,
+        in_specs=[pl.BlockSpec(memory_space=pltpu.MemorySpace.HBM)] * 3,
         out_specs=(vmem,) * 3,
         scratch_shapes=[
+            pltpu.VMEM(volume.shape, BF16),
+            pltpu.VMEM(weights.shape, BF16),
+            pltpu.VMEM(grad_out.shape, BF16),
             pltpu.VMEM((chans + 1, count_s, count_h, half, size_z, 2 * ch), BF16),
-            pltpu.VMEM((count_s + 2, all_y + 2, size_z, total), BF16),
+            pltpu.VMEM((2, count_s + 2, all_y + 2, size_z, total // 2), BF16),
             pltpu.VMEM((count_s + 2, all_y + 2, size_z, wide), BF16),
-            pltpu.VMEM((count_s, 2 * count_h, wide, cells), BF16),
+            pltpu.VMEM((count_s, wide, 2 * count_h * cells), BF16),
             pltpu.VMEM((2, cells, total), F32),
             pltpu.VMEM((2 * chans, cells, 2 * ch), F32),
+            dma((3,)),
             dma((chans - 1,)), dma((chans - 1,)),
             dma((chans + 1, 8)), dma((chans + 1, 8)),
             dma((chans - 1,)), dma((chans - 1,)),
+            dma((5,)), dma((5,)),
         ],
         compiler_params=pltpu.CompilerParams(
             collective_id=0, has_side_effects=True, vmem_limit_bytes=50 * 2**20

time: 42.4 us -> 42.3 us (level)
  the two profiles are of different devices: /device:TPU:1 before, /device:TPU:0 now
where the time goes in v2:
time: 42.3 us; the launch traced here: 42.1 us
  Pallas kernels  36 us (85%)
  local copies, waits for them, and re-layouts  5.49 us (13%)
  between operations  0.65 us (2%)
    pallas_call x1, Pallas kernels, fused_body(): pl.pallas_call(functools.partial(fused_kernel, scale=scale), out_shape=(j...  36 us
    unnamed x9, local copies, waits for them, and re-layouts  5.49 us

profile of v2, /device:TPU:0, one launch (start us, length us, event | category | flops | bytes accessed | tf_op | source)
XLA Modules:
  0.0 42.1 jit_solution(10089717899328017363)
XLA Ops:
  0.6 0.0 copy-start
  0.6 1.2 %copy-done = bf16[27,64,256]{2,1,0:T(8,128)(2,1)S(1)} copy-done((bf16[27,64,256]{2,1,0:T(8,128)(2,1)S(1)}, bf16[27,64,256]{2,1,0:T(8,128)(2,1)}, u32[]{:S(2)}) %copy-start) | copy-done | bytes 884760
  1.8 0.0 copy-start.1
  1.8 0.9 %copy-done.1 = bf16[1,8,64,64]{3,2,1,0:T(8,128)(2,1)S(1)} copy-done((bf16[1,8,64,64]{3,2,1,0:T(8,128)(2,1)S(1)}, bf16[1,8,64,64]{3,2,1,0:T(8,128)(2,1)}, u32[]{:S(2)}) %copy-start.1) | copy-done | bytes 65560
  2.7 0.0 copy-start.2
  2.7 0.9 %copy-done.2 = bf16[1,8,64,64]{3,2,1,0:T(8,128)(2,1)S(1)} copy-done((bf16[1,8,64,64]{3,2,1,0:T(8,128)(2,1)S(1)}, bf16[1,8,64,64]{3,2,1,0:T(8,128)(2,1)}, u32[]{:S(2)}) %copy-start.2) | copy-done | bytes 65560
  3.6 36.0 %shard_map.58 = (bf16[1,8,64,64]{3,2,1,0:T(8,128)(2,1)S(1)}, bf16[1,8,64,64]{3,2,1,0:T(8,128)(2,1)S(1)}, f32[9,192,256]{2,1,0:T(8,128)S(1)}) custom-call(bf16[1,8,64,64]{3,2,1,0:T(8,128)(2,1)S(1)} %copy-done.1, bf16[9,192,256]{2,1,0:T(8,128)(2,1)S(1)} %bitcast.3, bf16[1,8,64,64]{3,2,1,0:T(8,128)(2,1)S(1)} %copy-done.2), custom_call_target="tpu_custom_call" | custom-call | tf_op jit(solution)/shard_map/pallas_call | solution.py:338
  39.6 0.7 %copy.9 = bf16[1,8,64,64]{3,2,1,0:T(8,128)(2,1)} copy(bf16[1,8,64,64]{3,2,1,0:T(8,128)(2,1)S(1)} %get-tuple-element.12) | data formatting | bytes 131072
  40.2 0.7 %copy.10 = bf16[1,8,64,64]{3,2,1,0:T(8,128)(2,1)} copy(bf16[1,8,64,64]{3,2,1,0:T(8,128)(2,1)S(1)} %get-tuple-element.13) | data formatting | bytes 131072
  40.9 1.2 %copy.11 = f32[27,64,256]{2,1,0:T(8,128)} copy(f32[27,64,256]{2,1,0:T(8,128)S(1)} %bitcast.2) | data formatting | bytes 3538944
Async XLA Ops:
  0.6 1.2 %copy-start = (bf16[27,64,256]{2,1,0:T(8,128)(2,1)S(1)}, bf16[27,64,256]{2,1,0:T(8,128)(2,1)}, u32[]{:S(2)}) copy-start(bf16[27,64,256]{2,1,0:T(8,128)(2,1)} %param.4) | copy-start | bytes 2654212
  1.8 0.9 %copy-start.1 = (bf16[1,8,64,64]{3,2,1,0:T(8,128)(2,1)S(1)}, bf16[1,8,64,64]{3,2,1,0:T(8,128)(2,1)}, u32[]{:S(2)}) copy-start(bf16[1,8,64,64]{3,2,1,0:T(8,128)(2,1)} %vol_hbm.1) | copy-start | bytes 196612
  2.7 0.9 %copy-start.2 = (bf16[1,8,64,64]{3,2,1,0:T(8,128)(2,1)S(1)}, bf16[1,8,64,64]{3,2,1,0:T(8,128)(2,1)}, u32[]{:S(2)}) copy-start(bf16[1,8,64,64]{3,2,1,0:T(8,128)(2,1)} %g_hbm.1) | copy-start | bytes 196612

commit v3 on v2

--- a/solution.py
+++ b/solution.py
@@ -117,19 +117,17 @@
         pl.semaphore_signal(barrier, inc=1, device_id=where, device_id_type=MESH)
 
     zero_row = jnp.zeros((2, size_z, total // 2), BF16)
-    zero_v = jnp.zeros((size_z, wide), BF16)
-    last_x, last_y = v3.shape[0] - 1, v3.shape[1] - 1
+    last_x, last_y = gpad.shape[1] - 1, gpad.shape[2] - 1
 
     @pl.loop(0, last_y + 1)
     def _(y):
         for x in (0, last_x):
             gpad[:, x, y] = zero_row
-            v3[x, y] = zero_v
 
     for x in range(1, last_x):
         for y in (0, last_y):
             gpad[:, x, y] = zero_row
-            v3[x, y] = zero_v
+    v3[...] = jnp.zeros(v3.shape, BF16)
 
     loads[0].wait()
     loads[1].wait()
@@ -179,44 +177,52 @@
         push(blocks.at[c, s, h], z_send.at[j], z_recv.at[j], {"chan": d})
     offer(1, c)
 
+    def shifted(block):
+        wide_block = block.astype(F32)
+        row = lax.broadcasted_iota(jnp.int32, block.shape, 0) % size_z
+        before = jnp.where(row == 0, 0.0, pltpu.roll(wide_block, 1, 0))
+        after = jnp.where(row == size_z - 1, 0.0, pltpu.roll(wide_block, block.shape[0] - 1, 0))
+        return before.astype(BF16), block, after.astype(BF16)
+
+    def spread(dx, x):
+        parts = shifted(blocks[chans, x, h].reshape(cells, 2 * ch))
+        parts = [moved.reshape(half, size_z, 2 * ch) for moved in parts]
+        for k in range(2):
+            v3[dx, 1 + k * half : 1 + (k + 1) * half] = jnp.concatenate(
+                [moved[:, :, k * ch : (k + 1) * ch] for moved in parts], axis=-1
+            )
+
+    def spread_edge(dx, x):
+        for side, (piece, lanes, row_at) in enumerate(
+            ((0, slice(0, ch), rows_y + 1), (half - 1, slice(ch, 2 * ch), 0))
+        ):
+            @pl.when(h == side)
+            def _():
+                parts = shifted(blocks[chans, x, 1 - side, piece])
+                v3[dx, row_at] = jnp.concatenate([moved[:, lanes] for moved in parts], axis=-1)
+
+    spread(1, s)
     relay(0, chans)
     relay(1, c)
     corner(0, chans)
+    from_core(0, chans)
+    spread_edge(1, s)
+    for dx in (0, 2):
+        @pl.when((s + dx >= 1) & (s + dx <= count_s))
+        def _():
+            spread(dx, s + dx - 1)
+            spread_edge(dx, s + dx - 1)
+
     from_chan(0)
     corner(1, c)
-    from_core(0, chans)
-    relay(2, others[0])
-    from_chan(1)
-
-    row = lax.broadcasted_iota(jnp.int32, (cells, 2 * ch), 0) % size_z
-
-    def shifted(x, hy):
-        centre = blocks[chans, x, hy].reshape(cells, 2 * ch).astype(F32)
-        before = jnp.where(row == 0, 0.0, pltpu.roll(centre, 1, 0))
-        after = jnp.where(row == size_z - 1, 0.0, pltpu.roll(centre, cells - 1, 0))
-        return before.astype(BF16), centre.astype(BF16), after.astype(BF16)
-
-    @pl.loop(0, count_s * count_h)
-    def _(n):
-        x, hy = n // count_h, n % count_h
-        parts = [moved.reshape(half, size_z, 2 * ch) for moved in shifted(x, hy)]
-        for k in range(2):
-            v3[x + 1, pl.ds(1 + hy * rows_y + k * half, half)] = jnp.concatenate(
-                [moved[:, :, k * ch : (k + 1) * ch] for moved in parts], axis=-1
-            )
-
-    corner(2, others[0])
-    relay(3, others[1])
-    from_chan(2)
     loads[2].wait()
 
-    for t in range(2):
-        acc = jnp.zeros((cells, total), F32)
-        for a in range(3):
-            for b in range(3):
-                window = v3[s + a, pl.ds(h * rows_y + t * half + b, half)].reshape(cells, wide)
-                acc = acc + jnp.dot(window, w_ref[3 * a + b], preferred_element_type=F32)
-        part[t] = acc
+    acc = jnp.zeros((2 * cells, total), F32)
+    for a in range(3):
+        for b in range(3):
+            window = v3[a, b : b + rows_y].reshape(2 * cells, wide)
+            acc = acc + jnp.dot(window, w_ref[3 * a + b], preferred_element_type=F32)
+    part[...] = acc.reshape(2, cells, total)
 
     for d in range(chans):
         for k in range(2):
@@ -225,19 +231,27 @@
     for j, d in enumerate(others):
         push(got.at[chans + d], r_send.at[j], r_recv.at[j], {"chan": d}, dst=got.at[c])
 
-    corner(3, others[1])
-    relay(4, others[2])
-
-    @pl.loop(0, count_s * count_h)
-    def _(n):
+    relay(2, others[0])
+    from_chan(1)
+    corner(2, others[0])
+    from_chan(2)
+    relay(3, others[1])
+
+    def turn(n):
         x, hy = n // count_h, n % count_h
-        for e, moved in enumerate(shifted(x, hy)):
+        for e, moved in enumerate(shifted(blocks[chans, x, hy].reshape(cells, 2 * ch))):
             turned = moved.T
             for k in range(2):
                 at = pl.multiple_of((hy * 2 + k) * cells, cells)
                 vt[x, e * ch : (e + 1) * ch, pl.ds(at, cells)] = turned[k * ch : (k + 1) * ch]
 
+    turns = count_s * count_h
+    pl.loop(0, turns // 4)(turn)
+    corner(3, others[1])
+    relay(4, others[2])
+    pl.loop(turns // 4, turns // 2)(turn)
     corner(4, others[2])
+    pl.loop(turns // 2, turns)(turn)
 
     def fill(pair):
         @pl.loop(0, count_s * count_h)
@@ -289,22 +303,18 @@
         4, 4, [(x, x + 1, 1) for x in range(count_s)], pl.multiple_of(core_at * top, top), top
     )
 
-    row_out = lax.broadcasted_iota(jnp.int32, (cells, ch), 0) % size_z
-    for t in range(2):
-        acc = jnp.zeros((cells, wide), F32)
-        for a in range(3):
-            for b in range(3):
-                window = cotangent(s + 2 - a, h * rows_y + t * half + 2 - b, half)
-                acc = acc + lax.dot_general(
-                    window, w_ref[3 * a + b],
-                    (((1,), (1,)), ((), ())), preferred_element_type=F32,
-                )
-        first, middle, final = acc[:, :ch], acc[:, ch : 2 * ch], acc[:, 2 * ch :]
-        later = jnp.where(row_out == size_z - 1, 0.0, pltpu.roll(first, cells - 1, 0))
-        sooner = jnp.where(row_out == 0, 0.0, pltpu.roll(final, 1, 0))
-        gi_ref[0, pl.ds(t * half, half)] = (
-            (later + middle + sooner).astype(BF16).reshape(half, size_z, ch)
-        )
+    row_out = lax.broadcasted_iota(jnp.int32, (2 * cells, ch), 0) % size_z
+    acc = jnp.zeros((2 * cells, wide), F32)
+    for a in range(3):
+        for b in range(3):
+            acc = acc + lax.dot_general(
+                cotangent(s + 2 - a, h * rows_y + 2 - b, rows_y), w_ref[3 * a + b],
+                (((1,), (1,)), ((), ())), preferred_element_type=F32,
+            )
+    first, middle, final = acc[:, :ch], acc[:, ch : 2 * ch], acc[:, 2 * ch :]
+    later = jnp.where(row_out == size_z - 1, 0.0, pltpu.roll(first, 2 * cells - 1, 0))
+    sooner = jnp.where(row_out == 0, 0.0, pltpu.roll(final, 1, 0))
+    gi_ref[0] = (later + middle + sooner).astype(BF16).reshape(rows_y, size_z, ch)
 
     for j, d in enumerate(others):
         arrived(got.at[d], r_send.at[j], r_recv.at[j], {"chan": d})
@@ -350,7 +360,7 @@
             pltpu.VMEM(grad_out.shape, BF16),
             pltpu.VMEM((chans + 1, count_s, count_h, half, size_z, 2 * ch), BF16),
             pltpu.VMEM((2, count_s + 2, all_y + 2, size_z, total // 2), BF16),
-            pltpu.VMEM((count_s + 2, all_y + 2, size_z, wide), BF16),
+            pltpu.VMEM((3, rows_y + 2, size_z, wide), BF16),
             pltpu.VMEM((count_s, wide, 2 * count_h * cells), BF16),
             pltpu.VMEM((2, cells, total), F32),
             pltpu.VMEM((2 * chans, cells, 2 * ch), F32),
@@ -361,7 +371,7 @@
             dma((5,)), dma((5,)),
         ],
         compiler_params=pltpu.CompilerParams(
-            collective_id=0, has_side_effects=True, vmem_limit_bytes=50 * 2**20
+            collective_id=0, has_side_effects=True, vmem_limit_bytes=60 * 2**20
         ),
     )(volume, weights, grad_out)
     return out, gi, gk.reshape(kernel.shape)

time: 42.3 us -> 43.8 us (1.035)
  Pallas kernels: 36 us -> 37 us
  local copies, waits for them, and re-layouts: 5.49 us -> 6.01 us
    pallas_call x1, Pallas kernels: 36 us -> 37 us  [fused_body(): pl.pallas_call(functools.partial(fused_kernel, scale=scale), out_shape=(j...]
    unnamed x9 -> x3, local copies, waits for them, and re-layouts: 5.49 us -> 6.01 us
where the time goes in v3:
time: 43.8 us; the launch traced here: 43.6 us
  Pallas kernels  37 us (84%)
  local copies, waits for them, and re-layouts  6.01 us (14%)
  between operations  0.64 us (1%)
    pallas_call x1, Pallas kernels, fused_body(): pl.pallas_call(functools.partial(fused_kernel, scale=scale), out_shape=(j...  37 us
    unnamed x3, local copies, waits for them, and re-layouts  6.01 us

profile of v3, /device:TPU:0, one launch (start us, length us, event | category | flops | bytes accessed | tf_op | source)
XLA Modules:
  0.0 43.6 jit_solution(12567605243451184216)
XLA Ops:
  0.6 37.0 %shard_map.58 = (bf16[1,8,64,64]{3,2,1,0:T(8,128)(2,1)}, bf16[1,8,64,64]{3,2,1,0:T(8,128)(2,1)}, f32[9,192,256]{2,1,0:T(8,128)}) custom-call(bf16[1,8,64,64]{3,2,1,0:T(8,128)(2,1)} %vol_hbm.1, bf16[9,192,256]{2,1,0:T(8,128)(2,1)} %bitcast.3, bf16[1,8,64,64]{3,2,1,0:T(8,128)(2,1)} %g_hbm.1), custom_call_target="tpu_custom_call" | custom-call | tf_op jit(solution)/shard_map/pallas_call | solution.py:348
  37.6 1.6 %copy.9 = bf16[1,8,64,64]{3,2,1,0:T(8,128)(2,1)} copy(bf16[1,8,64,64]{3,2,1,0:T(8,128)(2,1)} %get-tuple-element.12) | data formatting | bytes 131072
  39.2 1.6 %copy.10 = bf16[1,8,64,64]{3,2,1,0:T(8,128)(2,1)} copy(bf16[1,8,64,64]{3,2,1,0:T(8,128)(2,1)} %get-tuple-element.13) | data formatting | bytes 131072
  40.7 2.9 %copy.11 = f32[27,64,256]{2,1,0:T(8,128)} copy(f32[27,64,256]{2,1,0:T(8,128)} %bitcast.2) | data formatting | bytes 3538944

commit v4 on v3

--- a/solution.py
+++ b/solution.py
@@ -73,11 +73,18 @@
 BF16 = jnp.bfloat16
 
 
-def fused_kernel(
-    vol_hbm, w_hbm, g_hbm, out_ref, gi_ref, gk_ref,
-    vol_ref, w_ref, g_ref, blocks, gpad, v3, vt, part, got,
-    in_sem, z_send, z_recv, p_send, p_recv, r_send, r_recv, k_send, k_recv,
-    *, scale,
+def shifted(block, size_z):
+    wide_block = block.astype(F32)
+    row = lax.broadcasted_iota(jnp.int32, block.shape, 0) % size_z
+    before = jnp.where(row == 0, 0.0, pltpu.roll(wide_block, 1, 0))
+    after = jnp.where(row == size_z - 1, 0.0, pltpu.roll(wide_block, block.shape[0] - 1, 0))
+    return before.astype(BF16), block, after.astype(BF16)
+
+
+def gather_kernel(
+    vol_hbm, w_hbm, g_hbm, out_ref, blocks,
+    vol_ref, w_ref, g_ref, v3, part, got,
+    in_sem, z_send, z_recv, p_send, p_recv, r_send, r_recv,
 ):
     chans, count_s, count_h = lax.axis_size("chan"), lax.axis_size("sx"), lax.axis_size("sy")
     c, s, h = lax.axis_index("chan"), lax.axis_index("sx"), lax.axis_index("sy")
@@ -116,17 +123,6 @@
     for where in partners:
         pl.semaphore_signal(barrier, inc=1, device_id=where, device_id_type=MESH)
 
-    zero_row = jnp.zeros((2, size_z, total // 2), BF16)
-    last_x, last_y = gpad.shape[1] - 1, gpad.shape[2] - 1
-
-    @pl.loop(0, last_y + 1)
-    def _(y):
-        for x in (0, last_x):
-            gpad[:, x, y] = zero_row
-
-    for x in range(1, last_x):
-        for y in (0, last_y):
-            gpad[:, x, y] = zero_row
     v3[...] = jnp.zeros(v3.shape, BF16)
 
     loads[0].wait()
@@ -177,15 +173,8 @@
         push(blocks.at[c, s, h], z_send.at[j], z_recv.at[j], {"chan": d})
     offer(1, c)
 
-    def shifted(block):
-        wide_block = block.astype(F32)
-        row = lax.broadcasted_iota(jnp.int32, block.shape, 0) % size_z
-        before = jnp.where(row == 0, 0.0, pltpu.roll(wide_block, 1, 0))
-        after = jnp.where(row == size_z - 1, 0.0, pltpu.roll(wide_block, block.shape[0] - 1, 0))
-        return before.astype(BF16), block, after.astype(BF16)
-
     def spread(dx, x):
-        parts = shifted(blocks[chans, x, h].reshape(cells, 2 * ch))
+        parts = shifted(blocks[chans, x, h].reshape(cells, 2 * ch), size_z)
         parts = [moved.reshape(half, size_z, 2 * ch) for moved in parts]
         for k in range(2):
             v3[dx, 1 + k * half : 1 + (k + 1) * half] = jnp.concatenate(
@@ -198,7 +187,7 @@
         ):
             @pl.when(h == side)
             def _():
-                parts = shifted(blocks[chans, x, 1 - side, piece])
+                parts = shifted(blocks[chans, x, 1 - side, piece], size_z)
                 v3[dx, row_at] = jnp.concatenate([moved[:, lanes] for moved in parts], axis=-1)
 
     spread(1, s)
@@ -237,21 +226,54 @@
     from_chan(2)
     relay(3, others[1])
 
+    corner(3, others[1])
+    relay(4, others[2])
+    corner(4, others[2])
+    for k, index in enumerate((c,) + others):
+        from_core(k + 1, index)
+
+    for j, d in enumerate(others):
+        arrived(got.at[d], r_send.at[j], r_recv.at[j], {"chan": d})
+    summed = got[chans + c]
+    for d in others:
+        summed = summed + got[d]
+    narrow = summed.astype(BF16).reshape(half, size_z, 2 * ch)
+    out_ref[0, :half] = narrow[:, :, :ch]
+    out_ref[0, half:] = narrow[:, :, ch:]
+
+    for copy in sent:
+        copy.wait_send()
+
+
+def gradient_kernel(blocks, w_ref, gi_ref, gk_ref, gpad, vt, *, scale):
+    chans, count_s, count_h = lax.axis_size("chan"), lax.axis_size("sx"), lax.axis_size("sy")
+    s, h = lax.axis_index("sx"), lax.axis_index("sy")
+    _, rows_y, size_z, ch = gi_ref.shape
+    half = rows_y // 2
+    cells = half * size_z
+    total = w_ref.shape[2]
+    wide = 3 * ch
+
+    zero_row = jnp.zeros((2, size_z, total // 2), BF16)
+    last_x, last_y = gpad.shape[1] - 1, gpad.shape[2] - 1
+
+    @pl.loop(0, last_y + 1)
+    def _(y):
+        for x in (0, last_x):
+            gpad[:, x, y] = zero_row
+
+    for x in range(1, last_x):
+        for y in (0, last_y):
+            gpad[:, x, y] = zero_row
     def turn(n):
         x, hy = n // count_h, n % count_h
-        for e, moved in enumerate(shifted(blocks[chans, x, hy].reshape(cells, 2 * ch))):
+        for e, moved in enumerate(shifted(blocks[chans, x, hy].reshape(cells, 2 * ch), size_z)):
             turned = moved.T
             for k in range(2):
                 at = pl.multiple_of((hy * 2 + k) * cells, cells)
                 vt[x, e * ch : (e + 1) * ch, pl.ds(at, cells)] = turned[k * ch : (k + 1) * ch]
 
-    turns = count_s * count_h
-    pl.loop(0, turns // 4)(turn)
-    corner(3, others[1])
-    relay(4, others[2])
-    pl.loop(turns // 4, turns // 2)(turn)
-    corner(4, others[2])
-    pl.loop(turns // 2, turns)(turn)
+    pl.loop(0, count_s * count_h)(turn)
 
     def fill(pair):
         @pl.loop(0, count_s * count_h)
@@ -264,44 +286,14 @@
                     [one[:, :, lanes], two[:, :, lanes]], axis=-1
                 )
 
-    from_core(1, c)
-    from_core(2, others[0])
-    fill(c // 2)
-    from_core(3, others[1])
-    from_core(4, others[2])
-    fill(1 - c // 2)
+    fill(0)
+    fill(1)
 
     def cotangent(x, start, rows):
         return jnp.concatenate(
             [gpad[p, x, pl.ds(start, rows)].reshape(rows * size_z, total // 2) for p in range(2)],
             axis=-1,
         )
-
-    core_at = s % 2
-    all_y = rows_y * count_h
-    top = wide // 2
-
-    def weight_gradient(step, index, terms, at, rows):
-        acc = jnp.zeros((rows, total), F32)
-        for x_in, x_out, start in terms:
-            acc = acc + jnp.dot(
-                vt[x_in, pl.ds(at, rows), :], cotangent(x_out, start, all_y),
-                preferred_element_type=F32,
-            )
-        gk_ref[index, pl.ds(at, rows)] = acc / scale
-        push(gk_ref.at[index, pl.ds(at, rows)], k_send.at[step], k_recv.at[step], to_core)
-
-    for b in range(3):
-        weight_gradient(
-            b, 6 * core_at + b,
-            [(x + core_at, x + 2 - core_at, 2 - b) for x in range(count_s - 1)], 0, wide,
-        )
-    weight_gradient(
-        3, 3 + 2 * core_at, [(x, x + 1, 2 - 2 * core_at) for x in range(count_s)], 0, wide
-    )
-    weight_gradient(
-        4, 4, [(x, x + 1, 1) for x in range(count_s)], pl.multiple_of(core_at * top, top), top
-    )
 
     row_out = lax.broadcasted_iota(jnp.int32, (2 * cells, ch), 0) % size_z
     acc = jnp.zeros((2 * cells, wide), F32)
@@ -316,22 +308,18 @@
     sooner = jnp.where(row_out == 0, 0.0, pltpu.roll(final, 1, 0))
     gi_ref[0] = (later + middle + sooner).astype(BF16).reshape(rows_y, size_z, ch)
 
-    for j, d in enumerate(others):
-        arrived(got.at[d], r_send.at[j], r_recv.at[j], {"chan": d})
-    summed = got[chans + c]
-    for d in others:
-        summed = summed + got[d]
-    narrow = summed.astype(BF16).reshape(half, size_z, 2 * ch)
-    out_ref[0, :half] = narrow[:, :, :ch]
-    out_ref[0, half:] = narrow[:, :, ch:]
-
-    for b in range(3):
-        arrived(gk_ref.at[6 * (1 - core_at) + b], k_send.at[b], k_recv.at[b], to_core)
-    arrived(gk_ref.at[5 - 2 * core_at], k_send.at[3], k_recv.at[3], to_core)
-    below = pl.multiple_of((1 - core_at) * top, top)
-    arrived(gk_ref.at[4, pl.ds(below, top)], k_send.at[4], k_recv.at[4], to_core)
-    for copy in sent:
-        copy.wait_send()
+    all_y = rows_y * count_h
+    for a in range(3):
+
+        @pl.loop(0, 3)
+        def _(b):
+            acc = jnp.zeros((wide, total), F32)
+            for x in range(count_s):
+                if 0 <= x + 1 - a < count_s:
+                    acc = acc + jnp.dot(
+                        vt[x], cotangent(x + 2 - a, 2 - b, all_y), preferred_element_type=F32
+                    )
+            gk_ref[3 * a + b] = acc / scale
 
 
 def fused_body(volume, kernel, grad_out):
@@ -344,36 +332,46 @@
     scale = math.sqrt(count_s * all_y * size_z)
     weights = kernel.reshape(9, wide, total)
     vmem = pl.BlockSpec(memory_space=pltpu.VMEM)
+    hbm = pl.BlockSpec(memory_space=pltpu.MemorySpace.HBM)
     dma = pltpu.SemaphoreType.DMA
-    out, gi, gk = pl.pallas_call(
-        functools.partial(fused_kernel, scale=scale),
+    out, blocks = pl.pallas_call(
+        gather_kernel,
         out_shape=(
             jax.ShapeDtypeStruct(volume.shape, BF16),
-            jax.ShapeDtypeStruct(volume.shape, BF16),
-            jax.ShapeDtypeStruct(weights.shape, F32),
+            jax.ShapeDtypeStruct((chans + 1, count_s, count_h, half, size_z, 2 * ch), BF16),
         ),
-        in_specs=[pl.BlockSpec(memory_space=pltpu.MemorySpace.HBM)] * 3,
-        out_specs=(vmem,) * 3,
+        in_specs=[hbm] * 3,
+        out_specs=(vmem, vmem),
         scratch_shapes=[
             pltpu.VMEM(volume.shape, BF16),
             pltpu.VMEM(weights.shape, BF16),
             pltpu.VMEM(grad_out.shape, BF16),
-            pltpu.VMEM((chans + 1, count_s, count_h, half, size_z, 2 * ch), BF16),
-            pltpu.VMEM((2, count_s + 2, all_y + 2, size_z, total // 2), BF16),
             pltpu.VMEM((3, rows_y + 2, size_z, wide), BF16),
-            pltpu.VMEM((count_s, wide, 2 * count_h * cells), BF16),
             pltpu.VMEM((2, cells, total), F32),
             pltpu.VMEM((2 * chans, cells, 2 * ch), F32),
             dma((3,)),
             dma((chans - 1,)), dma((chans - 1,)),
             dma((chans + 1, 8)), dma((chans + 1, 8)),
             dma((chans - 1,)), dma((chans - 1,)),
-            dma((5,)), dma((5,)),
         ],
         compiler_params=pltpu.CompilerParams(
-            collective_id=0, has_side_effects=True, vmem_limit_bytes=60 * 2**20
+            collective_id=0, has_side_effects=True, vmem_limit_bytes=40 * 2**20
         ),
     )(volume, weights, grad_out)
+    gi, gk = pl.pallas_call(
+        functools.partial(gradient_kernel, scale=scale),
+        out_shape=(
+            jax.ShapeDtypeStruct(volume.shape, BF16),
+            jax.ShapeDtypeStruct(weights.shape, F32),
+        ),
+        in_specs=[vmem] * 2,
+        out_specs=(vmem, vmem),
+        scratch_shapes=[
+            pltpu.VMEM((2, count_s + 2, all_y + 2, size_z, total // 2), BF16),
+            pltpu.VMEM((count_s, wide, 2 * count_h * cells), BF16),
+        ],
+        compiler_params=pltpu.CompilerParams(vmem_limit_bytes=40 * 2**20),
+    )(blocks, weights)
     return out, gi, gk.reshape(kernel.shape)
 
 

time: 43.8 us -> 44.7 us (1.021)
  Pallas kernels: 37 us -> 38.9 us
  local copies, waits for them, and re-layouts: 6.01 us -> 4.79 us
    pallas_call x1 -> x2, Pallas kernels: 37 us -> 38.9 us  [the longest x1 29.5 us: fused_body(): pl.pallas_call(gather_kernel, out_shape=(jax.ShapeDtypeStruct(volume.shap...]
    unnamed x3 -> x9, local copies, waits for them, and re-layouts: 6.01 us -> 4.79 us
where the time goes in v4:
time: 44.7 us; the launch traced here: 44.4 us
  Pallas kernels  38.9 us (87%)
  local copies, waits for them, and re-layouts  4.79 us (11%)
  between operations  0.66 us (1%)
    pallas_call x1, Pallas kernels, fused_body(): pl.pallas_call(gather_kernel, out_shape=(jax.ShapeDtypeStruct(volume.shap...  29.5 us
    pallas_call x1, Pallas kernels, fused_body(): pl.pallas_call(functools.partial(gradient_kernel, scale=scale), out_shape...  9.49 us
    unnamed x9, local copies, waits for them, and re-layouts  4.79 us

profile of v4, /device:TPU:0, one launch (start us, length us, event | category | flops | bytes accessed | tf_op | source)
XLA Modules:
  0.0 44.4 jit_solution(17230581192900636235)
XLA Ops:
  0.6 0.0 copy-start
  0.6 1.2 %copy-done = bf16[27,64,256]{2,1,0:T(8,128)(2,1)S(1)} copy-done((bf16[27,64,256]{2,1,0:T(8,128)(2,1)S(1)}, bf16[27,64,256]{2,1,0:T(8,128)(2,1)}, u32[]{:S(2)}) %copy-start) | copy-done | bytes 884760
  1.8 0.0 copy-start.2
  1.8 0.9 %copy-done.2 = bf16[1,8,64,64]{3,2,1,0:T(8,128)(2,1)S(1)} copy-done((bf16[1,8,64,64]{3,2,1,0:T(8,128)(2,1)S(1)}, bf16[1,8,64,64]{3,2,1,0:T(8,128)(2,1)}, u32[]{:S(2)}) %copy-start.2) | copy-done | bytes 65560
  2.7 0.0 copy-start.3
  2.7 0.9 %copy-done.3 = bf16[1,8,64,64]{3,2,1,0:T(8,128)(2,1)S(1)} copy-done((bf16[1,8,64,64]{3,2,1,0:T(8,128)(2,1)S(1)}, bf16[1,8,64,64]{3,2,1,0:T(8,128)(2,1)}, u32[]{:S(2)}) %copy-start.3) | copy-done | bytes 65560
  3.6 29.5 %shard_map.58 = (bf16[1,8,64,64]{3,2,1,0:T(8,128)(2,1)S(1)}, bf16[5,4,2,4,64,128]{5,4,3,2,1,0:T(8,128)(2,1)S(1)}) custom-call(bf16[1,8,64,64]{3,2,1,0:T(8,128)(2,1)S(1)} %copy-done.2, bf16[9,192,256]{2,1,0:T(8,128)(2,1)S(1)} %bitcast.2, bf16[1,8,64,64]{3,2,1,0:T(8,128)(2,1)S(1)} %copy-done.3), custom_call_target="tpu_custom_call" | custom-call | tf_op jit(solution)/shard_map/pallas_call | solution.py:337
  33.1 0.0 copy-start.1
  33.1 1.2 %copy-done.1 = bf16[27,64,256]{2,1,0:T(8,128)(2,1)S(1)} copy-done((bf16[27,64,256]{2,1,0:T(8,128)(2,1)S(1)}, bf16[27,64,256]{2,1,0:T(8,128)(2,1)}, u32[]{:S(2)}) %copy-start.1) | copy-done | bytes 884760
  34.2 9.5 %shard_map.59 = (bf16[1,8,64,64]{3,2,1,0:T(8,128)(2,1)}, f32[9,192,256]{2,1,0:T(8,128)}) custom-call(bf16[5,4,2,4,64,128]{5,4,3,2,1,0:T(8,128)(2,1)S(1)} %get-tuple-element.8.blocks, bf16[9,192,256]{2,1,0:T(8,128)(2,1)S(1)} %bitcast.3), custom_call_target="tpu_custom_call" | custom-call | tf_op jit(solution)/shard_map/pallas_call | solution.py:361
  43.7 0.7 %copy.7 = bf16[1,8,64,64]{3,2,1,0:T(8,128)(2,1)} copy(bf16[1,8,64,64]{3,2,1,0:T(8,128)(2,1)S(1)} %get-tuple-element.14) | data formatting | bytes 131072
Async XLA Ops:
  0.6 1.2 %copy-start = (bf16[27,64,256]{2,1,0:T(8,128)(2,1)S(1)}, bf16[27,64,256]{2,1,0:T(8,128)(2,1)}, u32[]{:S(2)}) copy-start(bf16[27,64,256]{2,1,0:T(8,128)(2,1)} %param.4) | copy-start | bytes 2654212
  1.8 0.9 %copy-start.2 = (bf16[1,8,64,64]{3,2,1,0:T(8,128)(2,1)S(1)}, bf16[1,8,64,64]{3,2,1,0:T(8,128)(2,1)}, u32[]{:S(2)}) copy-start(bf16[1,8,64,64]{3,2,1,0:T(8,128)(2,1)} %vol_hbm.1) | copy-start | bytes 196612
  2.7 0.9 %copy-start.3 = (bf16[1,8,64,64]{3,2,1,0:T(8,128)(2,1)S(1)}, bf16[1,8,64,64]{3,2,1,0:T(8,128)(2,1)}, u32[]{:S(2)}) copy-start(bf16[1,8,64,64]{3,2,1,0:T(8,128)(2,1)} %g_hbm.1) | copy-start | bytes 196612
  33.1 1.2 %copy-start.1 = (bf16[27,64,256]{2,1,0:T(8,128)(2,1)S(1)}, bf16[27,64,256]{2,1,0:T(8,128)(2,1)}, u32[]{:S(2)}) copy-start(bf16[27,64,256]{2,1,0:T(8,128)(2,1)} %param.4) | copy-start | bytes 2654212

commit v5 on v3

--- a/solution.py
+++ b/solution.py
@@ -74,20 +74,21 @@
 
 
 def fused_kernel(
-    vol_hbm, w_hbm, g_hbm, out_ref, gi_ref, gk_ref,
-    vol_ref, w_ref, g_ref, blocks, gpad, v3, vt, part, got,
-    in_sem, z_send, z_recv, p_send, p_recv, r_send, r_recv, k_send, k_recv,
+    in_ref, w_ref, out_ref, gi_ref, gk_ref,
+    blocks, gpad, v3, vt, part, from_near, from_far, side_block, side_rows,
+    z_send, z_recv, p_send, p_recv, r_send, r_recv, k_send, k_recv, s_send, s_recv,
     *, scale,
 ):
     chans, count_s, count_h = lax.axis_size("chan"), lax.axis_size("sx"), lax.axis_size("sy")
     c, s, h = lax.axis_index("chan"), lax.axis_index("sx"), lax.axis_index("sy")
-    rows_y, size_z, ch = vol_ref.shape[1:]
+    rows_y, size_z, ch = in_ref.shape[1:]
     half = rows_y // 2
     cells = half * size_z
     total = w_ref.shape[2]
     wide = 3 * ch
     core, far_s, far_h = s + 1 - 2 * (s % 2), (s + 2) % 4, 1 - h
     others = (c + 1 - 2 * (c % 2), (c + 2) % 4, 3 - c)
+    side = 3 - s
     to_x, to_y, to_core = {"sx": far_s}, {"sy": far_h}, {"sx": core}
     sent = []
 
@@ -105,14 +106,11 @@
     def arrived(ref, send, recv, where):
         remote(ref, ref, send, recv, where).wait_recv()
 
-    loads = [
-        pltpu.make_async_copy(src, dst, in_sem.at[k])
-        for k, (src, dst) in enumerate(((g_hbm, g_ref), (vol_hbm, vol_ref), (w_hbm, w_ref)))
-    ]
-    for load in loads:
-        load.start()
     barrier = pltpu.get_barrier_semaphore()
-    partners = [{"chan": d} for d in others] + [to_x, to_y, to_core]
+    to_side, to_side_row = {"sx": side}, {"sx": side, "sy": far_h}
+    to_core_row = {"sx": core, "sy": far_h}
+    partners = [{"chan": d} for d in others[:2]] + [to_x, to_y, to_core]
+    partners += [to_side, to_side_row, to_core_row]
     for where in partners:
         pl.semaphore_signal(barrier, inc=1, device_id=where, device_id_type=MESH)
 
@@ -129,11 +127,9 @@
             gpad[:, x, y] = zero_row
     v3[...] = jnp.zeros(v3.shape, BF16)
 
-    loads[0].wait()
-    loads[1].wait()
-    for index, ref in ((c, g_ref), (chans, vol_ref)):
-        blocks[index, s, h, :, :, :ch] = ref[0, :half]
-        blocks[index, s, h, :, :, ch:] = ref[0, half:]
+    for k, index in enumerate((chans, c)):
+        blocks[index, s, h, :, :, :ch] = in_ref[k, :half]
+        blocks[index, s, h, :, :, ch:] = in_ref[k, half:]
 
     pl.semaphore_wait(barrier, len(partners))
 
@@ -160,20 +156,35 @@
         arrived(diag.at[cut:], p_send.at[k, 4], p_recv.at[k, 4], to_x)
         push(diag, p_send.at[k, 7], p_recv.at[k, 7], to_core)
 
-    def from_core(k, index):
-        far_core = 3 - s
+    def near_core(k, index):
         arrived(blocks.at[index, core, h], p_send.at[k, 2], p_recv.at[k, 2], to_core)
-        arrived(blocks.at[index, far_core, h], p_send.at[k, 5], p_recv.at[k, 5], to_core)
+
+    def far_core(k, index):
+        arrived(blocks.at[index, side, h], p_send.at[k, 5], p_recv.at[k, 5], to_core)
         arrived(blocks.at[index, core, far_h], p_send.at[k, 6], p_recv.at[k, 6], to_core)
-        arrived(blocks.at[index, far_core, far_h], p_send.at[k, 7], p_recv.at[k, 7], to_core)
+        arrived(blocks.at[index, side, far_h], p_send.at[k, 7], p_recv.at[k, 7], to_core)
 
     def from_chan(j):
         index = others[j]
         arrived(blocks.at[index, s, h], z_send.at[j], z_recv.at[j], {"chan": index})
         offer(j + 2, index)
 
+    own, edge = blocks.at[chans, s, h], blocks.at[chans, s, h, (half - 1) * (1 - h)]
+    inner = (s >= 1) & (s <= count_s - 2)
+    side_copies = [
+        remote(own, side_block, s_send.at[0], s_recv.at[0], to_side),
+        remote(edge, side_rows.at[1], s_send.at[1], s_recv.at[1], to_side_row),
+    ]
+    core_row = remote(edge, side_rows.at[0], s_send.at[2], s_recv.at[2], to_core_row)
+    core_row.start()
+
+    @pl.when(inner)
+    def _():
+        for copy in side_copies:
+            copy.start()
+
     offer(0, chans)
-    for j, d in enumerate(others):
+    for j, d in enumerate(others[:2]):
         push(blocks.at[c, s, h], z_send.at[j], z_recv.at[j], {"chan": d})
     offer(1, c)
 
@@ -184,58 +195,72 @@
         after = jnp.where(row == size_z - 1, 0.0, pltpu.roll(wide_block, block.shape[0] - 1, 0))
         return before.astype(BF16), block, after.astype(BF16)
 
-    def spread(dx, x):
-        parts = shifted(blocks[chans, x, h].reshape(cells, 2 * ch))
+    def spread(dx, block):
+        parts = shifted(block.reshape(cells, 2 * ch))
         parts = [moved.reshape(half, size_z, 2 * ch) for moved in parts]
         for k in range(2):
             v3[dx, 1 + k * half : 1 + (k + 1) * half] = jnp.concatenate(
                 [moved[:, :, k * ch : (k + 1) * ch] for moved in parts], axis=-1
             )
 
-    def spread_edge(dx, x):
-        for side, (piece, lanes, row_at) in enumerate(
-            ((0, slice(0, ch), rows_y + 1), (half - 1, slice(ch, 2 * ch), 0))
-        ):
-            @pl.when(h == side)
+    def spread_edge(dx, rows):
+        parts = shifted(rows)
+        for at_h, lanes, row_at in ((0, slice(0, ch), rows_y + 1), (1, slice(ch, 2 * ch), 0)):
+            @pl.when(h == at_h)
             def _():
-                parts = shifted(blocks[chans, x, 1 - side, piece])
                 v3[dx, row_at] = jnp.concatenate([moved[:, lanes] for moved in parts], axis=-1)
 
-    spread(1, s)
+    spread(1, own[...])
     relay(0, chans)
+    near_core(0, chans)
+    core_row.wait()
+    dx_core, dx_side = 2 - 2 * (s % 2), 2 * (s % 2)
+    spread(dx_core, blocks[chans, core, h])
+    spread_edge(1, blocks[chans, s, far_h, (half - 1) * h])
+    spread_edge(dx_core, side_rows[0])
+
+    @pl.when(inner)
+    def _():
+        for copy in side_copies:
+            copy.wait()
+        spread(dx_side, side_block[...])
+        spread_edge(dx_side, side_rows[1])
+
+    from_chan(0)
+    from_chan(1)
+    push(blocks.at[others[1], s, h], z_send.at[2], z_recv.at[2], {"chan": others[0]})
+
+    for t in range(2):
+        acc = jnp.zeros((cells, total), F32)
+        for a in range(3):
+            for b in range(3):
+                window = v3[a, t * half + b : t * half + b + half].reshape(cells, wide)
+                acc = acc + jnp.dot(window, w_ref[3 * a + b], preferred_element_type=F32)
+        for d in range(chans):
+            for k in range(2):
+                part[d, t, :, k * ch : (k + 1) * ch] = (
+                    acc[k * cells // 2 : (k + 1) * cells // 2, d * ch : (d + 1) * ch]
+                )
+        for k, d in enumerate((others[0], others[2])):
+            push(
+                part.at[d, t], r_send.at[t, k], r_recv.at[t, k], {"chan": others[0]},
+                dst=from_near.at[k, t],
+            )
+
+    def pair_sum(t):
+        for k in (1, 0):
+            arrived(from_near.at[k, t], r_send.at[t, k], r_recv.at[t, k], {"chan": others[0]})
+        part[others[1], t] = part[others[1], t] + from_near[1, t]
+        push(
+            part.at[others[1], t], r_send.at[t, 2], r_recv.at[t, 2], {"chan": others[1]},
+            dst=from_far.at[t],
+        )
+
     relay(1, c)
     corner(0, chans)
-    from_core(0, chans)
-    spread_edge(1, s)
-    for dx in (0, 2):
-        @pl.when((s + dx >= 1) & (s + dx <= count_s))
-        def _():
-            spread(dx, s + dx - 1)
-            spread_edge(dx, s + dx - 1)
-
-    from_chan(0)
+    relay(2, others[0])
     corner(1, c)
-    loads[2].wait()
-
-    acc = jnp.zeros((2 * cells, total), F32)
-    for a in range(3):
-        for b in range(3):
-            window = v3[a, b : b + rows_y].reshape(2 * cells, wide)
-            acc = acc + jnp.dot(window, w_ref[3 * a + b], preferred_element_type=F32)
-    part[...] = acc.reshape(2, cells, total)
-
-    for d in range(chans):
-        for k in range(2):
-            got[chans + d, :, k * ch : (k + 1) * ch] = part[k, :, d * ch : (d + 1) * ch]
-
-    for j, d in enumerate(others):
-        push(got.at[chans + d], r_send.at[j], r_recv.at[j], {"chan": d}, dst=got.at[c])
-
-    relay(2, others[0])
-    from_chan(1)
-    corner(2, others[0])
-    from_chan(2)
-    relay(3, others[1])
+    far_core(0, chans)
 
     def turn(n):
         x, hy = n // count_h, n % count_h
@@ -247,11 +272,17 @@
 
     turns = count_s * count_h
     pl.loop(0, turns // 4)(turn)
+    from_chan(2)
+    relay(3, others[1])
+    corner(2, others[0])
+    pl.loop(turns // 4, turns // 2)(turn)
+    pair_sum(0)
+    pl.loop(turns // 2, 3 * turns // 4)(turn)
+    relay(4, others[2])
+    pair_sum(1)
+    pl.loop(3 * turns // 4, turns)(turn)
     corner(3, others[1])
-    relay(4, others[2])
-    pl.loop(turns // 4, turns // 2)(turn)
     corner(4, others[2])
-    pl.loop(turns // 2, turns)(turn)
 
     def fill(pair):
         @pl.loop(0, count_s * count_h)
@@ -264,12 +295,12 @@
                     [one[:, :, lanes], two[:, :, lanes]], axis=-1
                 )
 
-    from_core(1, c)
-    from_core(2, others[0])
-    fill(c // 2)
-    from_core(3, others[1])
-    from_core(4, others[2])
-    fill(1 - c // 2)
+    everything = list(enumerate((c,) + others, 1))
+    for now, pair in ((everything[:2], c // 2), (everything[2:], 1 - c // 2)):
+        for k, index in now:
+            near_core(k, index)
+            far_core(k, index)
+        fill(pair)
 
     def cotangent(x, start, rows):
         return jnp.concatenate(
@@ -316,14 +347,13 @@
     sooner = jnp.where(row_out == 0, 0.0, pltpu.roll(final, 1, 0))
     gi_ref[0] = (later + middle + sooner).astype(BF16).reshape(rows_y, size_z, ch)
 
-    for j, d in enumerate(others):
-        arrived(got.at[d], r_send.at[j], r_recv.at[j], {"chan": d})
-    summed = got[chans + c]
-    for d in others:
-        summed = summed + got[d]
-    narrow = summed.astype(BF16).reshape(half, size_z, 2 * ch)
-    out_ref[0, :half] = narrow[:, :, :ch]
-    out_ref[0, half:] = narrow[:, :, ch:]
+    for t in range(2):
+        arrived(from_far.at[t], r_send.at[t, 2], r_recv.at[t, 2], {"chan": others[1]})
+        summed = part[c, t] + from_near[0, t] + from_far[t]
+        narrow = summed.astype(BF16).reshape(half // 2, size_z, 2 * ch)
+        for k in range(2):
+            at = t * half + k * (half // 2)
+            out_ref[0, at : at + half // 2] = narrow[:, :, k * ch : (k + 1) * ch]
 
     for b in range(3):
         arrived(gk_ref.at[6 * (1 - core_at) + b], k_send.at[b], k_recv.at[b], to_core)
@@ -352,28 +382,28 @@
             jax.ShapeDtypeStruct(volume.shape, BF16),
             jax.ShapeDtypeStruct(weights.shape, F32),
         ),
-        in_specs=[pl.BlockSpec(memory_space=pltpu.MemorySpace.HBM)] * 3,
+        in_specs=[vmem] * 2,
         out_specs=(vmem,) * 3,
         scratch_shapes=[
-            pltpu.VMEM(volume.shape, BF16),
-            pltpu.VMEM(weights.shape, BF16),
-            pltpu.VMEM(grad_out.shape, BF16),
             pltpu.VMEM((chans + 1, count_s, count_h, half, size_z, 2 * ch), BF16),
             pltpu.VMEM((2, count_s + 2, all_y + 2, size_z, total // 2), BF16),
             pltpu.VMEM((3, rows_y + 2, size_z, wide), BF16),
             pltpu.VMEM((count_s, wide, 2 * count_h * cells), BF16),
-            pltpu.VMEM((2, cells, total), F32),
-            pltpu.VMEM((2 * chans, cells, 2 * ch), F32),
-            dma((3,)),
-            dma((chans - 1,)), dma((chans - 1,)),
+            pltpu.VMEM((chans, 2, cells // 2, 2 * ch), F32),
+            pltpu.VMEM((2, 2, cells // 2, 2 * ch), F32),
+            pltpu.VMEM((2, cells // 2, 2 * ch), F32),
+            pltpu.VMEM((half, size_z, 2 * ch), BF16),
+            pltpu.VMEM((2, size_z, 2 * ch), BF16),
+            dma((3,)), dma((3,)),
             dma((chans + 1, 8)), dma((chans + 1, 8)),
-            dma((chans - 1,)), dma((chans - 1,)),
+            dma((2, 3)), dma((2, 3)),
             dma((5,)), dma((5,)),
+            dma((3,)), dma((3,)),
         ],
         compiler_params=pltpu.CompilerParams(
-            collective_id=0, has_side_effects=True, vmem_limit_bytes=60 * 2**20
+            collective_id=0, has_side_effects=True, vmem_limit_bytes=50 * 2**20
         ),
-    )(volume, weights, grad_out)
+    )(jnp.concatenate([volume, grad_out]), weights)
     return out, gi, gk.reshape(kernel.shape)
 
 

time: 43.8 us -> 35 us (0.80)
  Pallas kernels: 37 us -> 29.5 us
  local copies, waits for them, and re-layouts: 6.01 us -> 3.68 us
  other arithmetic: 0 us -> 1.02 us
    pallas_call x1, Pallas kernels: 37 us -> 29.5 us  [fused_body(): pl.pallas_call(functools.partial(fused_kernel, scale=scale), out_shape=(j...]
    unnamed x3 -> x5, local copies, waits for them, and re-layouts: 6.01 us -> 3.68 us
    concatenate x0 -> x1, other arithmetic: none -> 1.02 us  [fused_body(): jnp.concatenate([volume, grad_out])]
where the time goes in v5:
time: 35 us; the launch traced here: 34.8 us
  Pallas kernels  29.5 us (84%)
  local copies, waits for them, and re-layouts  3.68 us (11%)
  other arithmetic  1.02 us (3%)
  between operations  0.65 us (2%)
    pallas_call x1, Pallas kernels, fused_body(): pl.pallas_call(functools.partial(fused_kernel, scale=scale), out_shape=(j...  29.5 us
    unnamed x5, local copies, waits for them, and re-layouts  3.68 us
    concatenate x1, other arithmetic, fused_body(): jnp.concatenate([volume, grad_out])  1.02 us

profile of v5, /device:TPU:0, one launch (start us, length us, event | category | flops | bytes accessed | tf_op | source)
XLA Modules:
  0.0 34.8 jit_solution(7210335458556188892)
XLA Ops:
  0.6 1.0 %pad_maximum_fusion.in_ref = bf16[2,8,64,64]{3,2,1,0:T(8,128)(2,1)S(1)} fusion(bf16[1,8,64,64]{3,2,1,0:T(8,128)(2,1)} %param.5, bf16[1,8,64,64]{3,2,1,0:T(8,128)(2,1)} %param.3), kind=kLoop, calls=%fused_computation | loop fusion | flops 65536 | bytes 262144 | tf_op jit(solution)/shard_map/concatenate | solution.py:406
  1.7 0.0 copy-start
  1.7 1.2 %copy-done = bf16[27,64,256]{2,1,0:T(8,128)(2,1)S(1)} copy-done((bf16[27,64,256]{2,1,0:T(8,128)(2,1)S(1)}, bf16[27,64,256]{2,1,0:T(8,128)(2,1)}, u32[]{:S(2)}) %copy-start) | copy-done | bytes 884760
  2.8 29.5 %shard_map.58 = (bf16[1,8,64,64]{3,2,1,0:T(8,128)(2,1)S(1)}, bf16[1,8,64,64]{3,2,1,0:T(8,128)(2,1)S(1)}, f32[9,192,256]{2,1,0:T(8,128)S(1)}) custom-call(bf16[2,8,64,64]{3,2,1,0:T(8,128)(2,1)S(1)} %pad_maximum_fusion.in_ref, bf16[9,192,256]{2,1,0:T(8,128)(2,1)S(1)} %bitcast.3), custom_call_target="tpu_custom_call" | custom-call | tf_op jit(solution)/shard_map/pallas_call | solution.py:378
  32.3 0.7 %copy.9 = bf16[1,8,64,64]{3,2,1,0:T(8,128)(2,1)} copy(bf16[1,8,64,64]{3,2,1,0:T(8,128)(2,1)S(1)} %get-tuple-element.12) | data formatting | bytes 131072
  33.0 0.7 %copy.10 = bf16[1,8,64,64]{3,2,1,0:T(8,128)(2,1)} copy(bf16[1,8,64,64]{3,2,1,0:T(8,128)(2,1)S(1)} %get-tuple-element.13) | data formatting | bytes 131072
  33.6 1.2 %copy.11 = f32[27,64,256]{2,1,0:T(8,128)} copy(f32[27,64,256]{2,1,0:T(8,128)S(1)} %bitcast.2) | data formatting | bytes 3538944
Async XLA Ops:
  1.7 1.2 %copy-start = (bf16[27,64,256]{2,1,0:T(8,128)(2,1)S(1)}, bf16[27,64,256]{2,1,0:T(8,128)(2,1)}, u32[]{:S(2)}) copy-start(bf16[27,64,256]{2,1,0:T(8,128)(2,1)} %param.4) | copy-start | bytes 2654212

commit v6 on v5

--- a/solution.py
+++ b/solution.py
@@ -271,19 +271,6 @@
                 vt[x, e * ch : (e + 1) * ch, pl.ds(at, cells)] = turned[k * ch : (k + 1) * ch]
 
     turns = count_s * count_h
-    pl.loop(0, turns // 4)(turn)
-    from_chan(2)
-    relay(3, others[1])
-    corner(2, others[0])
-    pl.loop(turns // 4, turns // 2)(turn)
-    pair_sum(0)
-    pl.loop(turns // 2, 3 * turns // 4)(turn)
-    relay(4, others[2])
-    pair_sum(1)
-    pl.loop(3 * turns // 4, turns)(turn)
-    corner(3, others[1])
-    corner(4, others[2])
-
     def fill(pair):
         @pl.loop(0, count_s * count_h)
         def _(n):
@@ -295,13 +282,6 @@
                     [one[:, :, lanes], two[:, :, lanes]], axis=-1
                 )
 
-    everything = list(enumerate((c,) + others, 1))
-    for now, pair in ((everything[:2], c // 2), (everything[2:], 1 - c // 2)):
-        for k, index in now:
-            near_core(k, index)
-            far_core(k, index)
-        fill(pair)
-
     def cotangent(x, start, rows):
         return jnp.concatenate(
             [gpad[p, x, pl.ds(start, rows)].reshape(rows * size_z, total // 2) for p in range(2)],
@@ -312,27 +292,63 @@
     all_y = rows_y * count_h
     top = wide // 2
 
-    def weight_gradient(step, index, terms, at, rows):
-        acc = jnp.zeros((rows, total), F32)
+    def weight_gradient(step, pair, index, terms, at, rows):
+        acc = jnp.zeros((rows, total // 2), F32)
         for x_in, x_out, start in terms:
+            window = gpad[pair, x_out, pl.ds(start, all_y)].reshape(all_y * size_z, total // 2)
             acc = acc + jnp.dot(
-                vt[x_in, pl.ds(at, rows), :], cotangent(x_out, start, all_y),
-                preferred_element_type=F32,
-            )
-        gk_ref[index, pl.ds(at, rows)] = acc / scale
-        push(gk_ref.at[index, pl.ds(at, rows)], k_send.at[step], k_recv.at[step], to_core)
-
-    for b in range(3):
-        weight_gradient(
-            b, 6 * core_at + b,
-            [(x + core_at, x + 2 - core_at, 2 - b) for x in range(count_s - 1)], 0, wide,
-        )
-    weight_gradient(
-        3, 3 + 2 * core_at, [(x, x + 1, 2 - 2 * core_at) for x in range(count_s)], 0, wide
-    )
-    weight_gradient(
-        4, 4, [(x, x + 1, 1) for x in range(count_s)], pl.multiple_of(core_at * top, top), top
-    )
+                vt[x_in, pl.ds(at, rows), :], window, preferred_element_type=F32
+            )
+        gk_ref[pair, index, pl.ds(at, rows)] = acc / scale
+        push(
+            gk_ref.at[pair, index, pl.ds(at, rows)],
+            k_send.at[step], k_recv.at[step], to_core,
+        )
+
+    def step_of(pair, first, step):
+        if step < 3:
+            weight_gradient(
+                first + step, pair, 6 * core_at + step,
+                [(x + core_at, x + 2 - core_at, 2 - step) for x in range(count_s - 1)], 0, wide,
+            )
+        elif step == 3:
+            weight_gradient(
+                first + step, pair, 3 + 2 * core_at,
+                [(x, x + 1, 2 - 2 * core_at) for x in range(count_s)], 0, wide,
+            )
+        else:
+            weight_gradient(
+                first + step, pair, 4, [(x, x + 1, 1) for x in range(count_s)],
+                pl.multiple_of(core_at * top, top), top,
+            )
+
+    pl.loop(0, turns // 2)(turn)
+    from_chan(2)
+    relay(3, others[1])
+    corner(2, others[0])
+    pl.loop(turns // 2, turns)(turn)
+
+    mine, other = c // 2, 1 - c // 2
+    for k, index in ((1, c), (2, others[0])):
+        near_core(k, index)
+        far_core(k, index)
+    fill(mine)
+    pair_sum(0)
+    step_of(mine, 0, 0)
+    step_of(mine, 0, 1)
+    relay(4, others[2])
+    step_of(mine, 0, 2)
+    pair_sum(1)
+    corner(3, others[1])
+    step_of(mine, 0, 3)
+    corner(4, others[2])
+    step_of(mine, 0, 4)
+    for k, index in ((3, others[1]), (4, others[2])):
+        near_core(k, index)
+        far_core(k, index)
+    fill(other)
+    for step in range(5):
+        step_of(other, 5, step)
 
     row_out = lax.broadcasted_iota(jnp.int32, (2 * cells, ch), 0) % size_z
     acc = jnp.zeros((2 * cells, wide), F32)
@@ -355,13 +371,28 @@
             at = t * half + k * (half // 2)
             out_ref[0, at : at + half // 2] = narrow[:, :, k * ch : (k + 1) * ch]
 
-    for b in range(3):
-        arrived(gk_ref.at[6 * (1 - core_at) + b], k_send.at[b], k_recv.at[b], to_core)
-    arrived(gk_ref.at[5 - 2 * core_at], k_send.at[3], k_recv.at[3], to_core)
     below = pl.multiple_of((1 - core_at) * top, top)
-    arrived(gk_ref.at[4, pl.ds(below, top)], k_send.at[4], k_recv.at[4], to_core)
+    for first, pair in ((0, mine), (5, other)):
+        theirs = [gk_ref.at[pair, 6 * (1 - core_at) + b] for b in range(3)]
+        theirs += [gk_ref.at[pair, 5 - 2 * core_at], gk_ref.at[pair, 4, pl.ds(below, top)]]
+        for step, ref in enumerate(theirs):
+            arrived(ref, k_send.at[first + step], k_recv.at[first + step], to_core)
     for copy in sent:
         copy.wait_send()
+
+
+def store_kernel(out_in, gi_in, gk_in, out_ref, gi_ref, gk_ref, sem):
+    lanes = gk_in.shape[3]
+    copies = [
+        pltpu.make_async_copy(gk_in.at[p], gk_ref.at[:, :, pl.ds(p * lanes, lanes)], sem.at[p])
+        for p in range(2)
+    ]
+    copies.append(pltpu.make_async_copy(out_in, out_ref, sem.at[2]))
+    copies.append(pltpu.make_async_copy(gi_in, gi_ref, sem.at[3]))
+    for copy in copies:
+        copy.start()
+    for copy in copies:
+        copy.wait()
 
 
 def fused_body(volume, kernel, grad_out):
@@ -380,7 +411,7 @@
         out_shape=(
             jax.ShapeDtypeStruct(volume.shape, BF16),
             jax.ShapeDtypeStruct(volume.shape, BF16),
-            jax.ShapeDtypeStruct(weights.shape, F32),
+            jax.ShapeDtypeStruct((2, 9, wide, total // 2), F32),
         ),
         in_specs=[vmem] * 2,
         out_specs=(vmem,) * 3,
@@ -397,13 +428,24 @@
             dma((3,)), dma((3,)),
             dma((chans + 1, 8)), dma((chans + 1, 8)),
             dma((2, 3)), dma((2, 3)),
-            dma((5,)), dma((5,)),
+            dma((10,)), dma((10,)),
             dma((3,)), dma((3,)),
         ],
         compiler_params=pltpu.CompilerParams(
             collective_id=0, has_side_effects=True, vmem_limit_bytes=50 * 2**20
         ),
     )(jnp.concatenate([volume, grad_out]), weights)
+    out, gi, gk = pl.pallas_call(
+        store_kernel,
+        out_shape=(
+            jax.ShapeDtypeStruct(volume.shape, BF16),
+            jax.ShapeDtypeStruct(volume.shape, BF16),
+            jax.ShapeDtypeStruct(weights.shape, F32),
+        ),
+        in_specs=[vmem] * 3,
+        out_specs=(pl.BlockSpec(memory_space=pltpu.MemorySpace.HBM),) * 3,
+        scratch_shapes=[dma((4,))],
+    )(out, gi, gk)
     return out, gi, gk.reshape(kernel.shape)
 
 

time: 35 us -> 37 us (1.057)
  Pallas kernels: 29.5 us -> 31.4 us
    pallas_call x0 -> x1, Pallas kernels: none -> 2.94 us  [fused_body(): pl.pallas_call(store_kernel, out_shape=(jax.ShapeDtypeStruct(volume.shape...]
    pallas_call x1, Pallas kernels: 29.5 us -> 28.5 us  [fused_body(): pl.pallas_call(functools.partial(fused_kernel, scale=scale), out_shape=(j...]
    unnamed x5 -> x8, local copies, waits for them, and re-layouts: 3.68 us -> 3.68 us
where the time goes in v6:
time: 37 us; the launch traced here: 36.8 us
  Pallas kernels  31.4 us (85%)
  local copies, waits for them, and re-layouts  3.68 us (10%)
  other arithmetic  1.02 us (3%)
  between operations  0.66 us (2%)
    pallas_call x1, Pallas kernels, fused_body(): pl.pallas_call(functools.partial(fused_kernel, scale=scale), out_shape=(j...  28.5 us
    unnamed x8, local copies, waits for them, and re-layouts  3.68 us
    pallas_call x1, Pallas kernels, fused_body(): pl.pallas_call(store_kernel, out_shape=(jax.ShapeDtypeStruct(volume.shape...  2.94 us
    concatenate x1, other arithmetic, fused_body(): jnp.concatenate([volume, grad_out])  1.02 us

profile of v6, /device:TPU:0, one launch (start us, length us, event | category | flops | bytes accessed | tf_op | source)
XLA Modules:
  0.0 36.8 jit_solution(15005090298557408696)
XLA Ops:
  0.6 1.0 %pad_maximum_fusion.in_ref = bf16[2,8,64,64]{3,2,1,0:T(8,128)(2,1)S(1)} fusion(bf16[1,8,64,64]{3,2,1,0:T(8,128)(2,1)} %param.5, bf16[1,8,64,64]{3,2,1,0:T(8,128)(2,1)} %param.3), kind=kLoop, calls=%fused_computation | loop fusion | flops 65536 | bytes 262144 | tf_op jit(solution)/shard_map/concatenate | solution.py:437
  1.7 0.0 copy-start.1
  1.7 1.2 %copy-done.1 = bf16[27,64,256]{2,1,0:T(8,128)(2,1)S(1)} copy-done((bf16[27,64,256]{2,1,0:T(8,128)(2,1)S(1)}, bf16[27,64,256]{2,1,0:T(8,128)(2,1)}, u32[]{:S(2)}) %copy-start.1) | copy-done | bytes 884760
  2.8 28.5 %shard_map.58 = (bf16[1,8,64,64]{3,2,1,0:T(8,128)(2,1)S(1)}, bf16[1,8,64,64]{3,2,1,0:T(8,128)(2,1)S(1)}, f32[2,9,192,128]{3,2,1,0:T(8,128)S(1)}) custom-call(bf16[2,8,64,64]{3,2,1,0:T(8,128)(2,1)S(1)} %pad_maximum_fusion.in_ref, bf16[9,192,256]{2,1,0:T(8,128)(2,1)S(1)} %bitcast.2), custom_call_target="tpu_custom_call" | custom-call | tf_op jit(solution)/shard_map/pallas_call | solution.py:409
  31.3 0.0 copy-start
  31.4 1.2 %copy-done = f32[2,9,192,128]{3,2,1,0:T(8,128)} copy-done((f32[2,9,192,128]{3,2,1,0:T(8,128)}, f32[2,9,192,128]{3,2,1,0:T(8,128)S(1)}, u32[]{:S(2)}) %copy-start) | copy-done | bytes 1769496
  32.6 0.0 copy-start.2
  32.6 0.6 %copy-done.2 = bf16[1,8,64,64]{3,2,1,0:T(8,128)(2,1)} copy-done((bf16[1,8,64,64]{3,2,1,0:T(8,128)(2,1)}, bf16[1,8,64,64]{3,2,1,0:T(8,128)(2,1)S(1)}, u32[]{:S(2)}) %copy-start.2) | copy-done | bytes 65560
  33.2 0.0 copy-start.3
  33.2 0.6 %copy-done.3 = bf16[1,8,64,64]{3,2,1,0:T(8,128)(2,1)} copy-done((bf16[1,8,64,64]{3,2,1,0:T(8,128)(2,1)}, bf16[1,8,64,64]{3,2,1,0:T(8,128)(2,1)S(1)}, u32[]{:S(2)}) %copy-start.3) | copy-done | bytes 65560
  33.9 2.9 %shard_map.59 = (bf16[1,8,64,64]{3,2,1,0:T(8,128)(2,1)}, bf16[1,8,64,64]{3,2,1,0:T(8,128)(2,1)}, f32[9,192,256]{2,1,0:T(8,128)}) custom-call(bf16[1,8,64,64]{3,2,1,0:T(8,128)(2,1)} %copy-done.2, bf16[1,8,64,64]{3,2,1,0:T(8,128)(2,1)} %copy-done.3, f32[2,9,192,128]{3,2,1,0:T(8,128)} %copy-done), custom_call_target="tpu_custom_call" | custom-call | tf_op jit(solution)/shard_map/pallas_call | solution.py:438
Async XLA Ops:
  1.7 1.2 %copy-start.1 = (bf16[27,64,256]{2,1,0:T(8,128)(2,1)S(1)}, bf16[27,64,256]{2,1,0:T(8,128)(2,1)}, u32[]{:S(2)}) copy-start(bf16[27,64,256]{2,1,0:T(8,128)(2,1)} %param.4) | copy-start | bytes 2654212
  31.3 1.2 %copy-start = (f32[2,9,192,128]{3,2,1,0:T(8,128)}, f32[2,9,192,128]{3,2,1,0:T(8,128)S(1)}, u32[]{:S(2)}) copy-start(f32[2,9,192,128]{3,2,1,0:T(8,128)S(1)} %get-tuple-element.11.gk_in) | copy-start | bytes 5308420
  32.6 0.6 %copy-start.2 = (bf16[1,8,64,64]{3,2,1,0:T(8,128)(2,1)}, bf16[1,8,64,64]{3,2,1,0:T(8,128)(2,1)S(1)}, u32[]{:S(2)}) copy-start(bf16[1,8,64,64]{3,2,1,0:T(8,128)(2,1)S(1)} %get-tuple-element.9.out_in) | copy-start | bytes 196612
  33.2 0.6 %copy-start.3 = (bf16[1,8,64,64]{3,2,1,0:T(8,128)(2,1)}, bf16[1,8,64,64]{3,2,1,0:T(8,128)(2,1)S(1)}, u32[]{:S(2)}) copy-start(bf16[1,8,64,64]{3,2,1,0:T(8,128)(2,1)S(1)} %get-tuple-element.10.gi_in) | copy-start | bytes 196612

commit v7 on v6

--- a/solution.py
+++ b/solution.py
@@ -75,7 +75,7 @@
 
 def fused_kernel(
     in_ref, w_ref, out_ref, gi_ref, gk_ref,
-    blocks, gpad, v3, vt, part, from_near, from_far, side_block, side_rows,
+    blocks, gpad, v3, vt, part, from_near, from_far, side_block, side_rows, back,
     z_send, z_recv, p_send, p_recv, r_send, r_recv, k_send, k_recv, s_send, s_recv,
     *, scale,
 ):
@@ -210,7 +210,19 @@
             def _():
                 v3[dx, row_at] = jnp.concatenate([moved[:, lanes] for moved in parts], axis=-1)
 
+    turns = count_s * count_h
+
+    def turn(i):
+        n = (s * count_h + h + i) % turns
+        x, hy = n // count_h, n % count_h
+        for e, moved in enumerate(shifted(blocks[chans, x, hy].reshape(cells, 2 * ch))):
+            turned = moved.T
+            for k in range(2):
+                at = pl.multiple_of((hy * 2 + k) * cells, cells)
+                vt[x, e * ch : (e + 1) * ch, pl.ds(at, cells)] = turned[k * ch : (k + 1) * ch]
+
     spread(1, own[...])
+    turn(0)
     relay(0, chans)
     near_core(0, chans)
     core_row.wait()
@@ -226,6 +238,7 @@
         spread(dx_side, side_block[...])
         spread_edge(dx_side, side_rows[1])
 
+    relay(1, c)
     from_chan(0)
     from_chan(1)
     push(blocks.at[others[1], s, h], z_send.at[2], z_recv.at[2], {"chan": others[0]})
@@ -256,21 +269,14 @@
             dst=from_far.at[t],
         )
 
-    relay(1, c)
+    from_chan(2)
+    relay(2, others[0])
+    relay(3, others[1])
     corner(0, chans)
-    relay(2, others[0])
     corner(1, c)
+    corner(2, others[0])
     far_core(0, chans)
 
-    def turn(n):
-        x, hy = n // count_h, n % count_h
-        for e, moved in enumerate(shifted(blocks[chans, x, hy].reshape(cells, 2 * ch))):
-            turned = moved.T
-            for k in range(2):
-                at = pl.multiple_of((hy * 2 + k) * cells, cells)
-                vt[x, e * ch : (e + 1) * ch, pl.ds(at, cells)] = turned[k * ch : (k + 1) * ch]
-
-    turns = count_s * count_h
     def fill(pair):
         @pl.loop(0, count_s * count_h)
         def _(n):
@@ -282,12 +288,6 @@
                     [one[:, :, lanes], two[:, :, lanes]], axis=-1
                 )
 
-    def cotangent(x, start, rows):
-        return jnp.concatenate(
-            [gpad[p, x, pl.ds(start, rows)].reshape(rows * size_z, total // 2) for p in range(2)],
-            axis=-1,
-        )
-
     core_at = s % 2
     all_y = rows_y * count_h
     top = wide // 2
@@ -322,11 +322,23 @@
                 pl.multiple_of(core_at * top, top), top,
             )
 
-    pl.loop(0, turns // 2)(turn)
-    from_chan(2)
-    relay(3, others[1])
-    corner(2, others[0])
+    pl.loop(1, turns // 2)(turn)
+    relay(4, others[2])
+    corner(3, others[1])
     pl.loop(turns // 2, turns)(turn)
+    corner(4, others[2])
+
+    def input_gradient(pair):
+        lanes = pl.ds(pl.multiple_of(pair * (total // 2), total // 2), total // 2)
+        acc = jnp.zeros((2 * cells, wide), F32)
+        for a in range(3):
+            for b in range(3):
+                window = gpad[pair, s + 2 - a, pl.ds(h * rows_y + 2 - b, rows_y)]
+                acc = acc + lax.dot_general(
+                    window.reshape(2 * cells, total // 2), w_ref[3 * a + b, :, lanes],
+                    (((1,), (1,)), ((), ())), preferred_element_type=F32,
+                )
+        return acc
 
     mine, other = c // 2, 1 - c // 2
     for k, index in ((1, c), (2, others[0])):
@@ -336,13 +348,11 @@
     pair_sum(0)
     step_of(mine, 0, 0)
     step_of(mine, 0, 1)
-    relay(4, others[2])
     step_of(mine, 0, 2)
     pair_sum(1)
-    corner(3, others[1])
     step_of(mine, 0, 3)
-    corner(4, others[2])
     step_of(mine, 0, 4)
+    back[...] = input_gradient(mine)
     for k, index in ((3, others[1]), (4, others[2])):
         near_core(k, index)
         far_core(k, index)
@@ -351,13 +361,7 @@
         step_of(other, 5, step)
 
     row_out = lax.broadcasted_iota(jnp.int32, (2 * cells, ch), 0) % size_z
-    acc = jnp.zeros((2 * cells, wide), F32)
-    for a in range(3):
-        for b in range(3):
-            acc = acc + lax.dot_general(
-                cotangent(s + 2 - a, h * rows_y + 2 - b, rows_y), w_ref[3 * a + b],
-                (((1,), (1,)), ((), ())), preferred_element_type=F32,
-            )
+    acc = back[...] + input_gradient(other)
     first, middle, final = acc[:, :ch], acc[:, ch : 2 * ch], acc[:, 2 * ch :]
     later = jnp.where(row_out == size_z - 1, 0.0, pltpu.roll(first, 2 * cells - 1, 0))
     sooner = jnp.where(row_out == 0, 0.0, pltpu.roll(final, 1, 0))
@@ -425,6 +429,7 @@
             pltpu.VMEM((2, cells // 2, 2 * ch), F32),
             pltpu.VMEM((half, size_z, 2 * ch), BF16),
             pltpu.VMEM((2, size_z, 2 * ch), BF16),
+            pltpu.VMEM((2 * cells, wide), F32),
             dma((3,)), dma((3,)),
             dma((chans + 1, 8)), dma((chans + 1, 8)),
             dma((2, 3)), dma((2, 3)),
@@ -445,6 +450,7 @@
         in_specs=[vmem] * 3,
         out_specs=(pl.BlockSpec(memory_space=pltpu.MemorySpace.HBM),) * 3,
         scratch_shapes=[dma((4,))],
+        compiler_params=pltpu.CompilerParams(vmem_limit_bytes=16 * 2**20),
     )(out, gi, gk)
     return out, gi, gk.reshape(kernel.shape)
 

time: 37 us -> 36.6 us (0.989)
  local copies, waits for them, and re-layouts: 3.68 us -> 1.16 us
  Pallas kernels: 31.4 us -> 33.5 us
    pallas_call x1, Pallas kernels: 28.5 us -> 32.2 us  [fused_body(): pl.pallas_call(functools.partial(fused_kernel, scale=scale), out_shape=(j...]
    unnamed x8 -> x2, local copies, waits for them, and re-layouts: 3.68 us -> 1.16 us
    pallas_call x1, Pallas kernels: 2.94 us -> 1.32 us  [fused_body(): pl.pallas_call(store_kernel, out_shape=(jax.ShapeDtypeStruct(volume.shape...]
where the time goes in v7:
time: 36.6 us; the launch traced here: 36.4 us
  Pallas kernels  33.5 us (92%)
  local copies, waits for them, and re-layouts  1.16 us (3%)
  other arithmetic  1.02 us (3%)
  between operations  0.65 us (2%)
    pallas_call x1, Pallas kernels, fused_body(): pl.pallas_call(functools.partial(fused_kernel, scale=scale), out_shape=(j...  32.2 us
    pallas_call x1, Pallas kernels, fused_body(): pl.pallas_call(store_kernel, out_shape=(jax.ShapeDtypeStruct(volume.shape...  1.32 us
    unnamed x2, local copies, waits for them, and re-layouts  1.16 us
    concatenate x1, other arithmetic, fused_body(): jnp.concatenate([volume, grad_out])  1.02 us

profile of v7, /device:TPU:0, one launch (start us, length us, event | category | flops | bytes accessed | tf_op | source)
XLA Modules:
  0.0 36.4 jit_solution(2722180309662632720)
XLA Ops:
  0.6 1.0 %pad_maximum_fusion.in_ref = bf16[2,8,64,64]{3,2,1,0:T(8,128)(2,1)S(1)} fusion(bf16[1,8,64,64]{3,2,1,0:T(8,128)(2,1)} %param.5, bf16[1,8,64,64]{3,2,1,0:T(8,128)(2,1)} %param.3), kind=kLoop, calls=%fused_computation | loop fusion | flops 65536 | bytes 262144 | tf_op jit(solution)/shard_map/concatenate | solution.py:442
  1.7 0.0 copy-start
  1.7 1.2 %copy-done = bf16[27,64,256]{2,1,0:T(8,128)(2,1)S(1)} copy-done((bf16[27,64,256]{2,1,0:T(8,128)(2,1)S(1)}, bf16[27,64,256]{2,1,0:T(8,128)(2,1)}, u32[]{:S(2)}) %copy-start) | copy-done | bytes 884760
  2.8 32.2 %shard_map.58 = (bf16[1,8,64,64]{3,2,1,0:T(8,128)(2,1)S(1)}, bf16[1,8,64,64]{3,2,1,0:T(8,128)(2,1)S(1)}, f32[2,9,192,128]{3,2,1,0:T(8,128)S(1)}) custom-call(bf16[2,8,64,64]{3,2,1,0:T(8,128)(2,1)S(1)} %pad_maximum_fusion.in_ref, bf16[9,192,256]{2,1,0:T(8,128)(2,1)S(1)} %bitcast.2), custom_call_target="tpu_custom_call" | custom-call | tf_op jit(solution)/shard_map/pallas_call | solution.py:413
  35.1 1.3 %shard_map.59 = (bf16[1,8,64,64]{3,2,1,0:T(8,128)(2,1)}, bf16[1,8,64,64]{3,2,1,0:T(8,128)(2,1)}, f32[9,192,256]{2,1,0:T(8,128)}) custom-call(bf16[1,8,64,64]{3,2,1,0:T(8,128)(2,1)S(1)} %get-tuple-element.9.out_in, bf16[1,8,64,64]{3,2,1,0:T(8,128)(2,1)S(1)} %get-tuple-element.10.gi_in, f32[2,9,192,128]{3,2,1,0:T(8,128)S(1)} %get-tuple-element.11.gk_in), custom_call_target="tpu_custom_call" | custom-call | tf_op jit(solution)/shard_map/pallas_call | solution.py:443
Async XLA Ops:
  1.7 1.2 %copy-start = (bf16[27,64,256]{2,1,0:T(8,128)(2,1)S(1)}, bf16[27,64,256]{2,1,0:T(8,128)(2,1)}, u32[]{:S(2)}) copy-start(bf16[27,64,256]{2,1,0:T(8,128)(2,1)} %param.4) | copy-start | bytes 2654212

commit v8 on v6

--- a/solution.py
+++ b/solution.py
@@ -445,6 +445,7 @@
         in_specs=[vmem] * 3,
         out_specs=(pl.BlockSpec(memory_space=pltpu.MemorySpace.HBM),) * 3,
         scratch_shapes=[dma((4,))],
+        compiler_params=pltpu.CompilerParams(vmem_limit_bytes=16 * 2**20),
     )(out, gi, gk)
     return out, gi, gk.reshape(kernel.shape)
 

time: 37 us -> 32.8 us (0.89)
  local copies, waits for them, and re-layouts: 3.68 us -> 1.16 us
  Pallas kernels: 31.4 us -> 29.8 us
    unnamed x8 -> x2, local copies, waits for them, and re-layouts: 3.68 us -> 1.16 us
    pallas_call x1, Pallas kernels: 2.94 us -> 1.32 us  [fused_body(): pl.pallas_call(store_kernel, out_shape=(jax.ShapeDtypeStruct(volume.shape...]
where the time goes in v8:
time: 32.8 us; the launch traced here: 32.7 us
  Pallas kernels  29.8 us (91%)
  local copies, waits for them, and re-layouts  1.16 us (4%)
  other arithmetic  1.02 us (3%)
  between operations  0.65 us (2%)
    pallas_call x1, Pallas kernels, fused_body(): pl.pallas_call(functools.partial(fused_kernel, scale=scale), out_shape=(j...  28.5 us
    pallas_call x1, Pallas kernels, fused_body(): pl.pallas_call(store_kernel, out_shape=(jax.ShapeDtypeStruct(volume.shape...  1.32 us
    unnamed x2, local copies, waits for them, and re-layouts  1.16 us
    concatenate x1, other arithmetic, fused_body(): jnp.concatenate([volume, grad_out])  1.02 us

profile of v8, /device:TPU:0, one launch (start us, length us, event | category | flops | bytes accessed | tf_op | source)
XLA Modules:
  0.0 32.7 jit_solution(5718491845438326235)
XLA Ops:
  0.6 1.0 %pad_maximum_fusion.in_ref = bf16[2,8,64,64]{3,2,1,0:T(8,128)(2,1)S(1)} fusion(bf16[1,8,64,64]{3,2,1,0:T(8,128)(2,1)} %param.5, bf16[1,8,64,64]{3,2,1,0:T(8,128)(2,1)} %param.3), kind=kLoop, calls=%fused_computation | loop fusion | flops 65536 | bytes 262144 | tf_op jit(solution)/shard_map/concatenate | solution.py:437
  1.7 0.0 copy-start
  1.7 1.2 %copy-done = bf16[27,64,256]{2,1,0:T(8,128)(2,1)S(1)} copy-done((bf16[27,64,256]{2,1,0:T(8,128)(2,1)S(1)}, bf16[27,64,256]{2,1,0:T(8,128)(2,1)}, u32[]{:S(2)}) %copy-start) | copy-done | bytes 884760
  2.8 28.5 %shard_map.58 = (bf16[1,8,64,64]{3,2,1,0:T(8,128)(2,1)S(1)}, bf16[1,8,64,64]{3,2,1,0:T(8,128)(2,1)S(1)}, f32[2,9,192,128]{3,2,1,0:T(8,128)S(1)}) custom-call(bf16[2,8,64,64]{3,2,1,0:T(8,128)(2,1)S(1)} %pad_maximum_fusion.in_ref, bf16[9,192,256]{2,1,0:T(8,128)(2,1)S(1)} %bitcast.2), custom_call_target="tpu_custom_call" | custom-call | tf_op jit(solution)/shard_map/pallas_call | solution.py:409
  31.3 1.3 %shard_map.59 = (bf16[1,8,64,64]{3,2,1,0:T(8,128)(2,1)}, bf16[1,8,64,64]{3,2,1,0:T(8,128)(2,1)}, f32[9,192,256]{2,1,0:T(8,128)}) custom-call(bf16[1,8,64,64]{3,2,1,0:T(8,128)(2,1)S(1)} %get-tuple-element.9.out_in, bf16[1,8,64,64]{3,2,1,0:T(8,128)(2,1)S(1)} %get-tuple-element.10.gi_in, f32[2,9,192,128]{3,2,1,0:T(8,128)S(1)} %get-tuple-element.11.gk_in), custom_call_target="tpu_custom_call" | custom-call | tf_op jit(solution)/shard_map/pallas_call | solution.py:438
Async XLA Ops:
  1.7 1.2 %copy-start = (bf16[27,64,256]{2,1,0:T(8,128)(2,1)S(1)}, bf16[27,64,256]{2,1,0:T(8,128)(2,1)}, u32[]{:S(2)}) copy-start(bf16[27,64,256]{2,1,0:T(8,128)(2,1)} %param.4) | copy-start | bytes 2654212

commit v9 on v8

--- a/solution.py
+++ b/solution.py
@@ -322,11 +322,13 @@
                 pl.multiple_of(core_at * top, top), top,
             )
 
-    pl.loop(0, turns // 2)(turn)
+    pl.loop(0, turns // 4)(turn)
     from_chan(2)
     relay(3, others[1])
     corner(2, others[0])
-    pl.loop(turns // 2, turns)(turn)
+    pl.loop(turns // 4, turns)(turn)
+    relay(4, others[2])
+    corner(3, others[1])
 
     mine, other = c // 2, 1 - c // 2
     for k, index in ((1, c), (2, others[0])):
@@ -336,12 +338,10 @@
     pair_sum(0)
     step_of(mine, 0, 0)
     step_of(mine, 0, 1)
-    relay(4, others[2])
+    corner(4, others[2])
     step_of(mine, 0, 2)
     pair_sum(1)
-    corner(3, others[1])
     step_of(mine, 0, 3)
-    corner(4, others[2])
     step_of(mine, 0, 4)
     for k, index in ((3, others[1]), (4, others[2])):
         near_core(k, index)

time: 32.8 us -> 33.8 us (1.030)
  Pallas kernels: 29.8 us -> 30.8 us
    pallas_call x1, Pallas kernels: 28.5 us -> 29.5 us  [fused_body(): pl.pallas_call(functools.partial(fused_kernel, scale=scale), out_shape=(j...]
where the time goes in v9:
time: 33.8 us; the launch traced here: 33.7 us
  Pallas kernels  30.8 us (91%)
  local copies, waits for them, and re-layouts  1.16 us (3%)
  other arithmetic  1.02 us (3%)
  between operations  0.65 us (2%)
    pallas_call x1, Pallas kernels, fused_body(): pl.pallas_call(functools.partial(fused_kernel, scale=scale), out_shape=(j...  29.5 us
    pallas_call x1, Pallas kernels, fused_body(): pl.pallas_call(store_kernel, out_shape=(jax.ShapeDtypeStruct(volume.shape...  1.32 us
    unnamed x2, local copies, waits for them, and re-layouts  1.16 us
    concatenate x1, other arithmetic, fused_body(): jnp.concatenate([volume, grad_out])  1.02 us

profile of v9, /device:TPU:0, one launch (start us, length us, event | category | flops | bytes accessed | tf_op | source)
XLA Modules:
  0.0 33.7 jit_solution(11078513172152582496)
XLA Ops:
  0.6 1.0 %pad_maximum_fusion.in_ref = bf16[2,8,64,64]{3,2,1,0:T(8,128)(2,1)S(1)} fusion(bf16[1,8,64,64]{3,2,1,0:T(8,128)(2,1)} %param.5, bf16[1,8,64,64]{3,2,1,0:T(8,128)(2,1)} %param.3), kind=kLoop, calls=%fused_computation | loop fusion | flops 65536 | bytes 262144 | tf_op jit(solution)/shard_map/concatenate | solution.py:437
  1.7 0.0 copy-start
  1.7 1.2 %copy-done = bf16[27,64,256]{2,1,0:T(8,128)(2,1)S(1)} copy-done((bf16[27,64,256]{2,1,0:T(8,128)(2,1)S(1)}, bf16[27,64,256]{2,1,0:T(8,128)(2,1)}, u32[]{:S(2)}) %copy-start) | copy-done | bytes 884760
  2.8 29.5 %shard_map.58 = (bf16[1,8,64,64]{3,2,1,0:T(8,128)(2,1)S(1)}, bf16[1,8,64,64]{3,2,1,0:T(8,128)(2,1)S(1)}, f32[2,9,192,128]{3,2,1,0:T(8,128)S(1)}) custom-call(bf16[2,8,64,64]{3,2,1,0:T(8,128)(2,1)S(1)} %pad_maximum_fusion.in_ref, bf16[9,192,256]{2,1,0:T(8,128)(2,1)S(1)} %bitcast.2), custom_call_target="tpu_custom_call" | custom-call | tf_op jit(solution)/shard_map/pallas_call | solution.py:409
  32.3 1.3 %shard_map.59 = (bf16[1,8,64,64]{3,2,1,0:T(8,128)(2,1)}, bf16[1,8,64,64]{3,2,1,0:T(8,128)(2,1)}, f32[9,192,256]{2,1,0:T(8,128)}) custom-call(bf16[1,8,64,64]{3,2,1,0:T(8,128)(2,1)S(1)} %get-tuple-element.9.out_in, bf16[1,8,64,64]{3,2,1,0:T(8,128)(2,1)S(1)} %get-tuple-element.10.gi_in, f32[2,9,192,128]{3,2,1,0:T(8,128)S(1)} %get-tuple-element.11.gk_in), custom_call_target="tpu_custom_call" | custom-call | tf_op jit(solution)/shard_map/pallas_call | solution.py:438
Async XLA Ops:
  1.7 1.2 %copy-start = (bf16[27,64,256]{2,1,0:T(8,128)(2,1)S(1)}, bf16[27,64,256]{2,1,0:T(8,128)(2,1)}, u32[]{:S(2)}) copy-start(bf16[27,64,256]{2,1,0:T(8,128)(2,1)} %param.4) | copy-start | bytes 2654212
